TPU v7x, 32 devices: a whole 2x2x4 slice. The times are simulated.
32 devices in a mesh: group: 4 (over z), sub: 8 (over y, x, core).
Axes of the slice: x: 2, y: 2, z: 4, core: 2. Of those that a mesh axis runs over, the one named last changes fastest.
Arguments:
- adjoint: float32 [4, 256, 65536], P(None, None, ('group', 'sub')), may hold values from -6 to 6
- velocity: bfloat16 [3, 256, 65536], P(None, None, ('group', 'sub')), may hold values from -6 to 6
- face_speed: bfloat16 [216, 65536], P(None, ('group', 'sub')), may hold values from -6 to 6
- derivatives: bfloat16 [768, 256], replicated, may hold values from -0.375 to 0.375
- lift_operator: bfloat16 [256, 216], replicated, may hold values from -1 to 1
- emission_profile: bfloat16 [256, 32], replicated, may hold values from -0.046875 to 0.046875
- neighbours: int32 [6, 65536], P(None, ('group', 'sub')), may hold values from 0 to 2815, as said below
- sub_sends: int32 [4, 16384], P(None, ('group', 'sub')), may hold values from 0 to 2047, as said below
- group_sends: int32 [2, 8192], P(None, ('group', 'sub')), may hold values from 0 to 2047, as said below
- element_tile: int32 [65536], P(('group', 'sub')), may hold values from 0 to 1023
- tile_slot: int32 [1024], replicated, may hold values from 0 to 1023, as said below
Outputs:
- adjoint_next: float32 [4, 256, 65536], P(None, None, ('group', 'sub'))
- emission_grad: float32 [1024, 128], P(('group', 'sub'))
Inputs may be any that keep to these rules, and one draw needn't show every extreme that they name: `neighbours`: faces pair up symmetrically: face 2a + 1 of an element meets face 2a of exactly one element. Positions below 2048 name an element of the same partition; positions 2048 + r * 64 + j name slot j from partition r of the group, and are used only for faces 0 to 3; positions from 2560 on name the adjacent group's slots and are used only for faces 4 and 5. `sub_sends`: column (p * 8 + r) * 64 + j is partition p's slot j for partition r of its group. Between two distinct partitions of a group the same number of face pairs, 8 to 64, crosses in each of faces 0 and 1 and of faces 2 and 3, filling slots 0 onwards; in every group some pair has 64. Unused slots, and a partition's slots for itself, name element 0 and are read by nobody. `group_sends`: column p * 256 + j is partition p's slot j. Partitions of the same index q in adjacent groups share 256 // 2 to 256 face pairs, the same number for every group, filling slots 0 onwards; some q has 256. Unused slots name element 0 and are read by nobody. `tile_slot`: A permutation of the tiles onto the rows.
All inputs are finite; a program needn't handle non-finite values.
Results may differ from a plain program's by a relative error of at most 0.0032.
Values may be sent and summed in bfloat16 or wider, within the bound.
A program may use at most 192 MiB of HBM per device.

v0:
```python
import jax
import jax.numpy as jnp
import numpy as np
from jax import lax
from jax.sharding import PartitionSpec as P

ORDER = 5


SECTION = 0.125


def passed_along(value, axis, steps):
    count = lax.axis_size(axis)
    pairs = [(source, (source + steps) % count) for source in range(count)]
    return lax.ppermute(value, axis, pairs)


def face_table(order):
    edge_nodes = order + 1
    coords_a, coords_b = np.meshgrid(np.arange(edge_nodes), np.arange(edge_nodes), indexing="ij")
    coords_a = coords_a.reshape(-1)
    coords_b = coords_b.reshape(-1)
    face_rows = []
    for axis_id in range(3):
        for level_id in (0, edge_nodes - 1):
            fixed_col = coords_a * 0 + level_id
            if axis_id == 0:
                triple = (fixed_col, coords_a, coords_b)
            elif axis_id == 1:
                triple = (coords_a, fixed_col, coords_b)
            else:
                triple = (coords_a, coords_b, fixed_col)
            face_rows.append((triple[0] * edge_nodes + triple[1]) * edge_nodes + triple[2])
    return np.stack(face_rows).astype(np.int32)


def pool_take(local_traces, received_part, positions):
    pool_rows = jnp.concatenate([local_traces, received_part], axis=2)
    return jnp.take(pool_rows, positions, axis=2)


def on_device(
    adjoint,
    velocity,
    face_speed,
    derivatives,
    lift_operator,
    emission_profile,
    neighbours,
    sub_sends,
    group_sends,
    element_tile,
    tile_slot,
):
    species, node_count, elements = adjoint.shape
    face_rows = jnp.asarray(face_table(ORDER))
    face_nodes = face_rows.shape[1]
    sub_span = sub_sends.shape[1]
    adjoint_lowered = adjoint.astype(jnp.bfloat16)
    traces = adjoint_lowered[:, face_rows, :]
    sub_out = jnp.stack(
        [jnp.take(traces[:, face_id], sub_sends[face_id], axis=2) for face_id in range(4)]
    )
    received = lax.all_to_all(sub_out, "sub", split_axis=3, concat_axis=3, tiled=True)
    upward = jnp.take(traces[:, 5], group_sends[1], axis=2)
    downward = jnp.take(traces[:, 4], group_sends[0], axis=2)
    from_below = passed_along(upward, "group", 1)
    from_above = passed_along(downward, "group", -1)
    gradient_terms = jnp.einsum(
        "hv,avr->ahr", derivatives, adjoint_lowered, preferred_element_type=jnp.float32
    )
    volume = (
        velocity[0] * gradient_terms[:, :node_count]
        + velocity[1] * gradient_terms[:, node_count : 2 * node_count]
        + velocity[2] * gradient_terms[:, 2 * node_count :]
    )
    outside_list = []
    for face_id in range(6):
        trace_id = face_id ^ 1
        positions = neighbours[face_id]
        if trace_id < 4:
            outside_list.append(pool_take(traces[:, trace_id], received[trace_id], positions))
        else:
            group_part = from_below if trace_id == 5 else from_above
            shifted = jnp.where(positions >= elements, positions - sub_span, positions)
            outside_list.append(pool_take(traces[:, trace_id], group_part, shifted))
    outside = jnp.stack(outside_list, axis=1)
    upwind = jnp.maximum(face_speed.astype(jnp.float32), 0.0).reshape(6, face_nodes, elements)
    face_flux_values = (upwind * (outside.astype(jnp.float32) - traces.astype(jnp.float32))).astype(
        jnp.bfloat16
    )
    face_flux_values = face_flux_values.reshape(species, 6 * face_nodes, elements)
    lifted_values = jnp.einsum(
        "dq,wqx->wdx", lift_operator, face_flux_values, preferred_element_type=jnp.float32
    )
    adjoint_next = adjoint + SECTION * (volume + lifted_values)
    next_lowered = adjoint_next.astype(jnp.bfloat16)
    contribution = jnp.einsum(
        "qvx,vj->xqj", next_lowered, emission_profile, preferred_element_type=jnp.float32
    ).reshape(elements, -1)
    tile_rows = jnp.take(tile_slot, element_tile)
    partial_sums = jax.ops.segment_sum(contribution, tile_rows, num_segments=tile_slot.shape[0])
    group_block = lax.psum_scatter(partial_sums, "group", scatter_dimension=0, tiled=True)
    emission_grad = lax.psum_scatter(group_block, "sub", scatter_dimension=0, tiled=True)
    return (adjoint_next, emission_grad)


def solution(mesh):
    placed = (
        P(None, None, ("group", "sub")),
        P(None, None, ("group", "sub")),
        P(None, ("group", "sub")),
        P(),
        P(),
        P(),
        P(None, ("group", "sub")),
        P(None, ("group", "sub")),
        P(None, ("group", "sub")),
        P(("group", "sub")),
        P(),
    )
    return jax.shard_map(
        on_device,
        mesh=mesh,
        in_specs=placed,
        out_specs=(P(None, None, ("group", "sub")), P(("group", "sub"), None)),
        check_vma=False,
    )
```

profile of v0, /device:TPU:0, one launch (start us, length us, event | category | flops | bytes accessed | tf_op | source)
XLA Modules:
  0.0 449.0 jit_solution(2738465959182665671)
XLA Ops:
  8.2 10.8 %copy.140 = bf16[4,256,2048]{2,0,1:T(4,128)(2,1)} copy(f32[4,256,2048]{2,1,0:T(8,128)} %param.20) | data formatting | bytes 12582912 | tf_op args[0]
  19.0 12.1 %gather_fusion = bf16[216,4,2048]{2,1,0:T(4,128)(2,1)} fusion(bf16[4,256,2048]{2,0,1:T(4,128)(2,1)} %copy.140, s32[1024]{0:T(1024)S(1)} %pad_clamp_fusion.6), kind=kCustom, calls=%fused_computation.12 | custom fusion | bytes 7078752 | tf_op jit(solution)/shard_map/gather | solution.py:61
  31.1 5.9 %slice_bitcast_fusion = (bf16[4,36,2048]{2,0,1:T(4,128)(2,1)}, bf16[4,36,2048]{2,0,1:T(4,128)(2,1)}, bf16[4,36,2048]{2,0,1:T(4,128)(2,1)S(1)}, bf16[4,36,2048]{2...) fusion(bf16[4,6,36,2048]{3,0,2,1:T(4,128)(2,1)} %bitcast.110), kind=kLoop, calls=%fused_computation.43 | loop fusion | bytes 7077888 | tf_op jit(solution)/shard_map/squeeze | solution.py:87
  72.5 5.7 %reshape.210 = bf16[8,2,18432]{2,1,0:T(2,128)(2,1)} reshape(bf16[512,4,4,36]{3,2,1,0:T(4,128)(2,1)S(1)} %copy_bitcast_fusion) | data formatting | bytes 1179648
  78.2 5.3 %all-to-all-start = ((bf16[8,2,18432]{2,1,0:T(2,128)(2,1)}), bf16[8,2,18432]{2,1,0:T(2,128)(2,1)}, u32[]{:S(2)}, u32[]{:S(2)}) async-start(bf16[8,2,18432]{2,1,0:T(2,128)(2,1)} %reshape.210), calls=%async_computation | async-start | bytes 1179648 | tf_op jit(solution)/shard_map/all_to_all | solution.py:65
  102.1 4.8 %bitcast_convert_fusion.2 = (f32[256,2048]{1,0:T(8,128)}, f32[256,2048]{1,0:T(8,128)}, f32[256,2048]{1,0:T(8,128)}) fusion(bf16[3,256,2048]{2,1,0:T(8,128)(2,1)} %param.21), kind=kLoop, calls=%fused_computation.36 | loop fusion | flops 1572864 | bytes 9437184 | tf_op jit(solution)/shard_map/mul | solution.py:74
  106.9 12.4 %convolution_bitcast_fusion = f32[4,768,2048]{1,2,0:T(8,128)} fusion(bf16[4,256,2048]{2,0,1:T(4,128)(2,1)S(1)} %copy-done.3, bf16[768,256]{1,0:T(8,128)(2,1)S(1)} %copy-done), kind=kOutput, calls=%fused_computation.15 | convolution fusion | flops 3221225472 | bytes 29753344 | tf_op jit(solution)/shard_map/hv,avr->ahr/dot_general | solution.py:70
  119.3 8.6 %gather_fusion.1 = s32[2048]{0:T(1024)S(1)} fusion(s32[1024]{0:T(1024)S(1)} %copy-done.2, s32[2048]{0:T(1024)S(1)} %get-tuple-element.41), kind=kCustom, calls=%fused_computation.13 | custom fusion | bytes 24576 | tf_op jit(solution)/shard_map/jit(_take)/gather | solution.py:102
  127.9 8.7 %copy.126 = f32[4,256,2048]{1,2,0:T(8,128)} copy(f32[4,256,2048]{2,1,0:T(8,128)} %param.20) | data formatting | bytes 16777216 | tf_op args[0]
  146.6 4.7 %copy.119 = bf16[4,36,2304]{1,0,2:T(4,128)(2,1)} copy(bf16[4,36,2304]{2,0,1:T(4,128)(2,1)} %pad_maximum_fusion.5) | data formatting | bytes 1327104 | tf_op jit(solution)/shard_map/concatenate | solution.py:39
  151.3 16.1 %gather_fusion.11 = bf16[2048,4,36]{2,1,0:T(4,128)(2,1)} fusion(bf16[4,36,2304]{1,0,2:T(4,128)(2,1)} %copy.119, s32[2048]{0:T(1024)S(1)} %fusion.20), kind=kCustom, calls=%fused_computation.3.clone | custom fusion | bytes 1187840 | tf_op jit(solution)/shard_map/jit(_take)/gather | solution.py:40
  173.9 4.7 %copy.123 = bf16[4,36,2304]{1,0,2:T(4,128)(2,1)} copy(bf16[4,36,2304]{2,0,1:T(4,128)(2,1)} %pad_maximum_fusion.6) | data formatting | bytes 1327104 | tf_op jit(solution)/shard_map/concatenate | solution.py:39
  178.6 16.1 %gather_fusion.13 = bf16[2048,4,36]{2,1,0:T(4,128)(2,1)} fusion(bf16[4,36,2304]{1,0,2:T(4,128)(2,1)} %copy.123, s32[2048]{0:T(1024)S(1)} %fusion.21), kind=kCustom, calls=%fused_computation.11.clone | custom fusion | bytes 1187840 | tf_op jit(solution)/shard_map/jit(_take)/gather | solution.py:40
  194.7 4.3 copy.124
  199.0 8.4 %reshape.211 = bf16[512,4,4,36]{3,2,1,0:T(4,128)(2,1)} reshape(bf16[8,2,18432]{2,1,0:T(2,128)(2,1)} %all-to-all-done) | data formatting | bytes 1179648
  214.6 5.1 %copy.106 = bf16[4,36,2560]{1,0,2:T(4,128)(2,1)} copy(bf16[4,36,2560]{2,0,1:T(4,128)(2,1)} %pad_maximum_fusion.1) | data formatting | bytes 1474560 | tf_op jit(solution)/shard_map/concatenate | solution.py:39
  219.6 16.2 %gather_fusion.6 = bf16[2048,4,36]{2,1,0:T(4,128)(2,1)} fusion(bf16[4,36,2560]{1,0,2:T(4,128)(2,1)} %copy.106, s32[2048]{0:T(1024)S(1)} %get-tuple-element.42), kind=kCustom, calls=%fused_computation.1.clone | custom fusion | bytes 1187840 | tf_op jit(solution)/shard_map/jit(_take)/gather | solution.py:40
  243.8 4.9 %copy.109 = bf16[4,36,2560]{1,0,2:T(4,128)(2,1)} copy(bf16[4,36,2560]{2,0,1:T(4,128)(2,1)} %pad_maximum_fusion.2) | data formatting | bytes 1474560 | tf_op jit(solution)/shard_map/concatenate | solution.py:39
  248.7 16.2 %gather_fusion.7 = bf16[2048,4,36]{2,1,0:T(4,128)(2,1)} fusion(bf16[4,36,2560]{1,0,2:T(4,128)(2,1)} %copy.109, s32[2048]{0:T(1024)S(1)} %get-tuple-element.43), kind=kCustom, calls=%fused_computation.7.clone | custom fusion | bytes 1187840 | tf_op jit(solution)/shard_map/jit(_take)/gather | solution.py:40
  272.9 4.9 %copy.112 = bf16[4,36,2560]{1,0,2:T(4,128)(2,1)} copy(bf16[4,36,2560]{2,0,1:T(4,128)(2,1)} %pad_maximum_fusion.3) | data formatting | bytes 1474560 | tf_op jit(solution)/shard_map/concatenate | solution.py:39
  277.7 16.2 %gather_fusion.8 = bf16[2048,4,36]{2,1,0:T(4,128)(2,1)} fusion(bf16[4,36,2560]{1,0,2:T(4,128)(2,1)} %copy.112, s32[2048]{0:T(1024)S(1)} %get-tuple-element.44), kind=kCustom, calls=%fused_computation.8.clone | custom fusion | bytes 1187840 | tf_op jit(solution)/shard_map/jit(_take)/gather | solution.py:40
  300.8 4.9 %copy.115 = bf16[4,36,2560]{1,0,2:T(4,128)(2,1)} copy(bf16[4,36,2560]{2,0,1:T(4,128)(2,1)} %pad_maximum_fusion.4) | data formatting | bytes 1474560 | tf_op jit(solution)/shard_map/concatenate | solution.py:39
  305.7 16.2 %gather_fusion.9 = bf16[2048,4,36]{2,1,0:T(4,128)(2,1)} fusion(bf16[4,36,2560]{1,0,2:T(4,128)(2,1)} %copy.115, s32[2048]{0:T(1024)S(1)} %fusion.19), kind=kCustom, calls=%fused_computation.9.clone | custom fusion | bytes 1187840 | tf_op jit(solution)/shard_map/jit(_take)/gather | solution.py:40
  321.9 4.3 copy.116
  330.2 4.4 convert_subtract_fusion
  334.6 7.3 %fusion.5 = bf16[4,216,2048]{2,0,1:T(4,128)(2,1)} fusion(f32[4,6,36,2048]{3,0,2,1:T(4,128)} %bitcast.112, f32[216,2048]{1,0:T(8,128)} %convert_maximum_fusion), kind=kLoop, calls=%fused_computation.26 | loop fusion | flops 3538944 | bytes 12386304 | tf_op jit(solution)/shard_map/convert_element_type | solution.py:90
  341.9 25.4 %fusion.3 = f32[4,256,2048]{1,2,0:T(8,128)} fusion(f32[4,256,2048]{1,2,0:T(8,128)} %copy.126, f32[4,768,2048]{1,2,0:T(8,128)} %convolution_bitcast_fusion, f32[256,2048]{0,1:T(8,128)} %copy.99, f32[256,2048]{0,1:T(8,128)} %copy.98, f32[256,2048]{0,1:T(8,128)S(1)} %copy.95, bf16[4,216,2048]{2,0,1:T(4,128)(2,1)} %fusion.5, bf16[256,216]{0,1:T(8,128)(2,1)S(1)} %copy-done.15), kind=kOutput, calls=%fused_computation.20 | convolution fusion | flops 922746880 | bytes 51884032 | tf_op jit(solution)/shard_map/dq,wqx->wdx/dot_general | solution.py:94
  367.4 4.7 %fusion.7 = f32[4,2048,32]{1,2,0:T(8,128)S(1)} fusion(f32[4,256,2048]{1,2,0:T(8,128)} %fusion.3, bf16[256,32]{0,1:T(8,128)(2,1)S(1)} %copy-done.18), kind=kOutput, calls=%fused_computation.29 | convolution fusion | flops 136314880 | bytes 9453568 | tf_op jit(solution)/shard_map/qvx,vj->xqj/dot_general | solution.py:99
  372.4 12.2 %scatter_custom_fusion = f32[1024,128]{1,0:T(8,128)} fusion(s32[2048]{0:T(1024)S(1)} %and_select_fusion, f32[2048,128]{1,0:T(8,128)S(1)} %copy.128, f32[]{:T(128)} %constant.33.clone.1), kind=kCustom, calls=%fused_computation.60 | custom fusion | flops 262144 | bytes 524292 | tf_op jit(solution)/shard_map/scatter-add | solution.py:103
  384.7 21.7 %reduce-scatter.3.cloned.1.call-done = f32[256,128]{1,0:T(8,128)} async-done(((f32[1024,128]{1,0:T(8,128)}), f32[256,128]{1,0:T(8,128)}) %reduce-scatter.3.cloned.1.call-update) | async-done | bytes 131088 | tf_op jit(solution)/shard_map/reduce_scatter | solution.py:104
  406.5 8.7 %copy.129 = f32[4,256,2048]{2,1,0:T(8,128)} copy(f32[4,256,2048]{1,2,0:T(8,128)} %fusion.3) | data formatting | bytes 16777216
  415.2 26.5 %reduce-scatter.5.cloned.1.call-done = f32[32,128]{1,0:T(8,128)} async-done(((f32[256,128]{1,0:T(8,128)}), f32[32,128]{1,0:T(8,128)}) %reduce-scatter.5.cloned.1.call-update) | async-done | bytes 16400 | tf_op jit(solution)/shard_map/reduce_scatter | solution.py:105
  (129 shorter events, 105.7 us)
Async XLA Ops:
  7.2 99.8 %copy-start = (bf16[768,256]{1,0:T(8,128)(2,1)S(1)}, bf16[768,256]{1,0:T(8,128)(2,1)}, u32[]{:S(2)}) copy-start(bf16[768,256]{1,0:T(8,128)(2,1)} %param.23) | copy-start | bytes 1179652
  8.1 10.8 %copy-start.20 = (s32[216]{0:T(256)S(1)}, s32[216]{0:T(256)}, u32[]{:S(2)}) copy-start(s32[216]{0:T(256)} %constant.77) | copy-start | bytes 2596
  37.0 5.6 %copy-start.5 = (bf16[4,36,2048]{2,0,1:T(4,128)(2,1)}, bf16[4,36,2048]{2,0,1:T(4,128)(2,1)S(1)}, u32[]{:S(2)}) copy-start(bf16[4,36,2048]{2,0,1:T(4,128)(2,1)S(1)} %get-tuple-element.18) | copy-start | bytes 1769476
  37.0 5.6 %copy-start.7 = (bf16[4,36,2048]{2,0,1:T(4,128)(2,1)}, bf16[4,36,2048]{2,0,1:T(4,128)(2,1)S(1)}, u32[]{:S(2)}) copy-start(bf16[4,36,2048]{2,0,1:T(4,128)(2,1)S(1)} %get-tuple-element.21) | copy-start | bytes 1769476
  37.0 8.3 %copy-start.6 = (bf16[4,36,2048]{2,0,1:T(4,128)(2,1)}, bf16[4,36,2048]{2,0,1:T(4,128)(2,1)S(1)}, u32[]{:S(2)}) copy-start(bf16[4,36,2048]{2,0,1:T(4,128)(2,1)S(1)} %get-tuple-element.20) | copy-start | bytes 1769476
  72.5 11.1 %copy-start.19 = (s32[2,256]{1,0:T(2,128)S(1)}, s32[2,256]{1,0:T(2,128)}, u32[]{:S(2)}) copy-start(s32[2,256]{1,0:T(2,128)} %param.28) | copy-start | bytes 6148
  78.2 14.5 %copy-start.8 = (bf16[4,36,2048]{2,0,1:T(4,128)(2,1)S(1)}, bf16[4,36,2048]{2,0,1:T(4,128)(2,1)}, u32[]{:S(2)}) copy-start(bf16[4,36,2048]{2,0,1:T(4,128)(2,1)} %get-tuple-element.16) | copy-start | bytes 1769476
  78.2 120.7 %all-to-all-start = ((bf16[8,2,18432]{2,1,0:T(2,128)(2,1)}), bf16[8,2,18432]{2,1,0:T(2,128)(2,1)}, u32[]{:S(2)}, u32[]{:S(2)}) async-start(bf16[8,2,18432]{2,1,0:T(2,128)(2,1)} %reshape.210), calls=%async_computation | async-start | bytes 1179648 | tf_op jit(solution)/shard_map/all_to_all | solution.py:65
  83.6 322.9 %reduce-scatter.3.cloned.1.call-start = ((), (), s32[]{:S(2)}) async-start(), calls=%async_computation.3 | async-start | bytes 655360 | tf_op jit(solution)/shard_map/reduce_scatter | solution.py:104
  87.7 12.7 %copy-start.16 = (s32[6,2048]{1,0:T(8,128)S(1)}, s32[6,2048]{1,0:T(8,128)}, u32[]{:S(2)}) copy-start(s32[6,2048]{1,0:T(8,128)} %param.26) | copy-start | bytes 147460
  87.7 12.8 %copy-start.17 = (s32[2048]{0:T(1024)S(1)}, s32[2048]{0:T(1024)}, u32[]{:S(2)}) copy-start(s32[2048]{0:T(1024)} %param.29) | copy-start | bytes 24580
  87.7 12.9 %copy-start.14 = (bf16[216,2048]{1,0:T(8,128)(2,1)S(1)}, bf16[216,2048]{1,0:T(8,128)(2,1)}, u32[]{:S(2)}) copy-start(bf16[216,2048]{1,0:T(8,128)(2,1)} %param.22) | copy-start | bytes 2654212
  90.7 53.7 %collective-permute-start = (bf16[4,36,256]{2,0,1:T(4,128)(2,1)S(1)}, bf16[4,36,256]{2,0,1:T(4,128)(2,1)S(1)}, u32[]{:S(2)}, u32[]{:S(2)}) collective-permute-start(bf16[4,36,256]{2,0,1:T(4,128)(2,1)S(1)} %select_bitcast_fusion.5), channel_id=1, source_target_pairs={{0,8},{8,16},{16,24},{24,0},{1,9},{9,17},{17,25},{25,1},{2,10},{10... | collective-permute-start | bytes 221192 | tf_op jit(solution)/shard_map/ppermute | solution.py:16
  98.3 73.4 %collective-permute-start.1 = (bf16[4,36,256]{2,0,1:T(4,128)(2,1)S(1)}, bf16[4,36,256]{2,0,1:T(4,128)(2,1)S(1)}, u32[]{:S(2)}, u32[]{:S(2)}) collective-permute-start(bf16[4,36,256]{2,0,1:T(4,128)(2,1)S(1)} %select_bitcast_fusion.4), channel_id=1, source_target_pairs={{0,24},{8,0},{16,8},{24,16},{1,25},{9,1},{17,9},{25,17},{2,26},{10... | collective-permute-start | bytes 221192 | tf_op jit(solution)/shard_map/ppermute | solution.py:16
  102.1 4.9 %copy-start.3 = (bf16[4,256,2048]{2,0,1:T(4,128)(2,1)S(1)}, bf16[4,256,2048]{2,0,1:T(4,128)(2,1)}, u32[]{:S(2)}) copy-start(bf16[4,256,2048]{2,0,1:T(4,128)(2,1)} %copy.140) | copy-start | bytes 12582916
  106.9 12.4 %copy-start.2 = (s32[1024]{0:T(1024)S(1)}, s32[1024]{0:T(1024)}, u32[]{:S(2)}) copy-start(s32[1024]{0:T(1024)} %param.30) | copy-start | bytes 12292
  305.6 20.5 %copy-start.11 = (bf16[2048,4,36]{0,1,2:T(4,128)(2,1)S(1)}, bf16[2048,4,36]{0,1,2:T(4,128)(2,1)}, u32[]{:S(2)}) copy-start(bf16[2048,4,36]{0,1,2:T(4,128)(2,1)} %copy.107) | copy-start | bytes 1769476
  326.2 2.0 copy-start.12
  326.2 2.5 copy-start.13
  326.2 2.9 copy-start.9
  326.6 2.9 copy-start.10
  328.2 2.0 copy-start.4
  334.6 7.3 %copy-start.15 = (bf16[256,216]{0,1:T(8,128)(2,1)S(1)}, bf16[256,216]{0,1:T(8,128)(2,1)}, u32[]{:S(2)}) copy-start(bf16[256,216]{0,1:T(8,128)(2,1)} %param.24) | copy-start | bytes 331780
  341.9 25.4 %copy-start.18 = (bf16[256,32]{0,1:T(8,128)(2,1)S(1)}, bf16[256,32]{0,1:T(8,128)(2,1)}, u32[]{:S(2)}) copy-start(bf16[256,32]{0,1:T(8,128)(2,1)} %param.25) | copy-start | bytes 49156
  384.7 57.1 %reduce-scatter.5.cloned.1.call-start = ((), (), s32[]{:S(2)}) async-start(), calls=%async_computation.4 | async-start | bytes 147456 | tf_op jit(solution)/shard_map/reduce_scatter | solution.py:105
  406.5 35.3 %copy-start.1 = (bf16[768,256]{1,0:T(8,128)(2,1)S(1)}, bf16[768,256]{1,0:T(8,128)(2,1)}, u32[]{:S(2)}) copy-start(bf16[768,256]{1,0:T(8,128)(2,1)} %param.23) | copy-start | bytes 1179652
Sparse Core Ops, SparseCore 0:
  384.8 21.6 reduce-scatter.2
  410.0 31.6 reduce-scatter.4
where the time goes:
time: 456 us; the launch traced here: 449 us
  local copies, waits for them, and re-layouts  275 us (60%)
  other arithmetic  59 us (13%)
  waiting for transfers between devices  48.3 us (11%)
  matrix products  42.5 us (9%)
  between operations  15 us (3%)
  starting transfers between devices  9.59 us (2%)
    gather x12, local copies, waits for them, and re-layouts, pool_take(): return jnp.take(pool_rows, positions, axis=2)  123 us
    unnamed x51, local copies, waits for them, and re-layouts  48.5 us
    concatenate x6, local copies, waits for them, and re-layouts, pool_take(): pool_rows = jnp.concatenate([local_traces, received_part], axis=2)  29 us
    reduce_scatter x1, waiting for transfers between devices, on_device(): lax.psum_scatter(group_block, 'sub', scatter_dimension=0, tiled=True)  26.5 us
    dot_general x1, matrix products, on_device(): jnp.einsum('dq,wqx->wdx', lift_operator, face_flux_values, preferred_elem...  25.4 us
    reduce_scatter x1, waiting for transfers between devices, on_device(): lax.psum_scatter(partial_sums, 'group', scatter_dimension=0, tiled=True)  21.7 us
    squeeze x3, local copies, waits for them, and re-layouts, on_device(): outside_list.append(pool_take(traces[:, trace_id], group_part, shifted))  12.7 us
    concatenate x6, other arithmetic, pool_take(): pool_rows = jnp.concatenate([local_traces, received_part], axis=2)  12.6 us
  transfers between devices with their start and end apart: 5, of which 2 were waited for; matrix products, arithmetic and copies ran while one was open for 27% of the time, Pallas kernels for 0%

commit v1 on v0

v1 whole, which is shorter than its diff:
```python
import functools

import jax
import jax.numpy as jnp
import numpy as np
from jax import lax
from jax.experimental import pallas as pl
from jax.experimental.pallas import tpu as pltpu
from jax.sharding import PartitionSpec as P

ORDER = 5
SECTION = 0.125
FACES = 6
SPAN = 256
MESH = pl.DeviceIdType.MESH
F32, BF16 = jnp.float32, jnp.bfloat16


def face_table(order):
    edge = order + 1
    a, b = np.meshgrid(np.arange(edge), np.arange(edge), indexing="ij")
    a, b = a.reshape(-1), b.reshape(-1)
    rows = []
    for axis_id in range(3):
        for level in (0, edge - 1):
            fixed = a * 0 + level
            i, j, l = [(fixed, a, b), (a, fixed, b), (a, b, fixed)][axis_id]
            rows.append((i * edge + j) * edge + l)
    return np.stack(rows).astype(np.int32)


def padded_nodes(face_nodes):
    return -(-face_nodes // 8) * 8


def select_matrix(node_count):
    table = face_table(ORDER)
    pad = padded_nodes(table.shape[1])
    out = np.zeros((FACES * pad, node_count), np.float32)
    for f in range(FACES):
        for k, n in enumerate(table[f]):
            out[f * pad + k, n] = 1
    return out


def spread_matrix(face_nodes):
    pad = padded_nodes(face_nodes)
    out = np.zeros((FACES * pad, FACES * face_nodes), np.float32)
    for f in range(FACES):
        for k in range(face_nodes):
            out[f * pad + k, f * face_nodes + k] = 1
    return out


def dot(a, b):
    return jnp.dot(a, b, preferred_element_type=F32)


def dot_nt(a, b):
    return lax.dot_general(a, b, (((1,), (1,)), ((), ())), preferred_element_type=F32)


def one_hot_rows(index, rows):
    ids = lax.broadcasted_iota(jnp.int32, (rows, index.shape[1]), 0)
    return jnp.where(ids == index, 1.0, 0.0).astype(BF16)


def columns_of(stack, position, first, count, block):
    picked = dot(stack, one_hot_rows(position & (SPAN - 1), SPAN))
    tile = position >> (SPAN.bit_length() - 1)
    out = jnp.zeros((block, position.shape[1]), F32)
    for t in range(count):
        out = jnp.where(tile == first + t, picked[t * block : (t + 1) * block], out)
    return out


def flux_kernel(
    n_group, n_sub, cap,
    adjoint, speed, neighbours, sub_sends, group_sends, select, spread,
    flux,
    field, table, local, send_sub, recv_sub, send_group, recv_group, far_sub,
    field_sem, sub_send_sem, sub_recv_sem, group_send_sem, group_recv_sem,
):
    tiles, species = field.shape[0], field.shape[1]
    pad = select.shape[0] // FACES
    block = species * pad
    elements = tiles * SPAN
    g, q = lax.axis_index("group"), lax.axis_index("sub")
    above = (lax.rem(g + 1, n_group), q)
    below = (lax.rem(g + n_group - 1, n_group), q)

    def field_copy(i):
        cols = pl.ds(pl.multiple_of(i * SPAN, SPAN), SPAN)
        return pltpu.make_async_copy(adjoint.at[:, :, cols], field.at[i], field_sem.at[i])

    for i in range(tiles):
        field_copy(i).start()

    barrier = pltpu.get_barrier_semaphore()
    peers = [(g, lax.rem(q + d, n_sub)) for d in range(1, n_sub)] + [above, below]
    for peer in peers:
        pl.semaphore_signal(barrier, inc=1, device_id=peer, device_id_type=MESH)

    def trace_tile(i, carry):
        field_copy(i).wait()
        parts = [dot(select[...], field[i, s].astype(BF16)) for s in range(species)]
        rows = pl.ds(pl.multiple_of(i * block, block), block)
        for f in range(FACES):
            one = jnp.concatenate([p[f * pad : (f + 1) * pad] for p in parts], axis=0)
            table[f, rows, :] = one.astype(BF16)
        return carry

    lax.fori_loop(0, tiles, trace_tile, 0)

    low_half = lax.broadcasted_iota(jnp.int32, (block, 2 * cap), 1) < cap
    for axis_id in range(2):
        for c in range(n_sub * cap // SPAN):
            cols = slice(c * SPAN, (c + 1) * SPAN)
            minus, plus = [
                columns_of(table[f], sub_sends[f : f + 1, cols], 0, tiles, block)
                for f in (2 * axis_id, 2 * axis_id + 1)
            ]
            for m in range(SPAN // (2 * cap)):
                part = slice(m * 2 * cap, (m + 1) * 2 * cap)
                a, b = minus[:, part], plus[:, part]
                r = c * (SPAN // cap) + 2 * m
                send_sub[r, axis_id] = jnp.where(low_half, a, pltpu.roll(b, cap, 1)).astype(BF16)
                send_sub[r + 1, axis_id] = jnp.where(low_half, pltpu.roll(a, cap, 1), b).astype(BF16)
    pl.semaphore_wait(barrier, len(peers))
    copies = []
    for d in range(1, n_sub):
        peer = lax.rem(q + d, n_sub)
        copies.append(
            pltpu.make_async_remote_copy(
                src_ref=send_sub.at[peer], dst_ref=recv_sub.at[q],
                send_sem=sub_send_sem.at[d], recv_sem=sub_recv_sem.at[d],
                device_id=(g, peer), device_id_type=MESH,
            )
        )
        copies[-1].start()
    span_group = send_group.shape[2]
    for k, target in ((0, below), (1, above)):
        for c in range(span_group // SPAN):
            cols = slice(c * SPAN, (c + 1) * SPAN)
            got = columns_of(table[4 + k], group_sends[k : k + 1, cols], 0, tiles, block)
            send_group[k, :, cols] = got.astype(BF16)
        copies.append(
            pltpu.make_async_remote_copy(
                src_ref=send_group.at[k], dst_ref=recv_group.at[k],
                send_sem=group_send_sem.at[k], recv_sem=group_recv_sem.at[k],
                device_id=target, device_id_type=MESH,
            )
        )
        copies[-1].start()
    recv_sub[q] = jnp.zeros(recv_sub.shape[1:], BF16)

    def local_tile(i, carry):
        cols = pl.ds(pl.multiple_of(i * SPAN, SPAN), SPAN)
        for f in range(FACES):
            got = columns_of(table[f ^ 1], neighbours[f : f + 1, cols], 0, tiles, block)
            local[f, :, cols] = got.astype(BF16)
        return carry

    lax.fori_loop(0, tiles, local_tile, 0)

    for copy in copies:
        copy.wait()
    far_tiles = n_sub * cap // SPAN
    for t in range(4):
        for r in range(0, n_sub, 2):
            a = recv_sub[r, t // 2].astype(F32)
            b = recv_sub[r + 1, t // 2].astype(F32)
            if t % 2 == 0:
                both = jnp.where(low_half, a, pltpu.roll(b, cap, 1))
            else:
                both = jnp.where(low_half, pltpu.roll(a, cap, 1), b)
            lane = r * cap
            far_sub[t, (lane // SPAN) * block : (lane // SPAN + 1) * block,
                    lane % SPAN : lane % SPAN + 2 * cap] = both.astype(BF16)

    def flux_tile(i, carry):
        cols = pl.ds(pl.multiple_of(i * SPAN, SPAN), SPAN)
        rows = pl.ds(pl.multiple_of(i * block, block), block)
        upwind = jnp.maximum(dot(spread[...], speed[:, cols]), 0.0)
        parts = []
        for f in range(FACES):
            t = f ^ 1
            position = neighbours[f : f + 1, cols]
            if t < 4:
                far = columns_of(far_sub[t], position, tiles, far_tiles, block)
            else:
                far = jnp.zeros((block, SPAN), F32)
                for c in range(span_group // SPAN):
                    got = recv_group[t - 4, :, c * SPAN : (c + 1) * SPAN]
                    far += columns_of(got, position, tiles + far_tiles + c, 1, block)
            outside = local[f, :, cols].astype(F32) + far
            wind = jnp.concatenate([upwind[f * pad : (f + 1) * pad]] * species, axis=0)
            parts.append(wind * (outside - table[f, rows, :].astype(F32)))
        for s in range(species):
            one = jnp.concatenate([p[s * pad : (s + 1) * pad] for p in parts], axis=0)
            flux[s, :, cols] = one.astype(BF16)
        return carry

    lax.fori_loop(0, tiles, flux_tile, 0)


def step_kernel(
    adjoint, velocity, flux, derivatives, lift, profile, spread, element_tile, tile_slot,
    adjoint_next, partial, lift_wide,
):
    species, nodes, span = adjoint.shape
    tile_rows = partial.shape[0]

    @pl.when(pl.program_id(0) == 0)
    def _():
        lift_wide[...] = dot_nt(lift[...], spread[...]).astype(BF16)
        partial[...] = jnp.zeros_like(partial)

    tile = element_tile[...]
    width = tile_slot.shape[1]
    slots = tile_slot[...]
    high = dot((slots >> 8).astype(F32).astype(BF16), one_hot_rows(lax.rem(tile, width), width))
    low = dot((slots & 255).astype(F32).astype(BF16), one_hot_rows(lax.rem(tile, width), width))
    picked = (high * 256.0 + low)
    which = lax.broadcasted_iota(jnp.int32, picked.shape, 0) == lax.div(tile, width)
    row = jnp.sum(jnp.where(which, picked, 0.0), axis=0, keepdims=True).astype(jnp.int32)

    contrib = []
    for s in range(species):
        field = adjoint[s]
        grads = dot(derivatives[...], field.astype(BF16))
        total = dot(lift_wide[...], flux[s])
        for d in range(3):
            total += velocity[d].astype(F32) * grads[d * nodes : (d + 1) * nodes]
        result = field + SECTION * total
        adjoint_next[s] = result
        contrib.append(lax.dot_general(
            profile[...], result.astype(BF16), (((0,), (0,)), ((), ())), preferred_element_type=F32))
    terms = jnp.concatenate(contrib, axis=0)
    first = terms.astype(BF16)
    second = (terms - first.astype(F32)).astype(BF16)
    both = jnp.concatenate([first, second], axis=0)
    sums = dot_nt(one_hot_rows(row, tile_rows), both)
    half = terms.shape[0]
    partial[...] += sums[:, :half] + sums[:, half:]


def sum_kernel(
    n_group, n_sub,
    partial, out,
    send, recv, mid, recv_mid,
    send_sem, recv_sem, mid_send_sem, mid_recv_sem,
):
    own = out.shape[0]
    g, q = lax.axis_index("group"), lax.axis_index("sub")
    barrier = pltpu.get_barrier_semaphore()
    peers = [(g, lax.rem(q + d, n_sub)) for d in range(1, n_sub)]
    peers += [(lax.rem(g + d, n_group), q) for d in range(1, n_group)]
    for peer in peers:
        pl.semaphore_signal(barrier, inc=1, device_id=peer, device_id_type=MESH)

    def rows_of(group, sub):
        return pl.ds(pl.multiple_of((group * n_sub + sub) * own, own), own)

    for d in range(1, n_sub):
        for k in range(n_group):
            send[d, k] = partial[rows_of(k, lax.rem(q + d, n_sub)), :].astype(BF16)
    pl.semaphore_wait(barrier, len(peers))
    copies = []
    for d in range(1, n_sub):
        copies.append(
            pltpu.make_async_remote_copy(
                src_ref=send.at[d], dst_ref=recv.at[d],
                send_sem=send_sem.at[d], recv_sem=recv_sem.at[d],
                device_id=(g, lax.rem(q + d, n_sub)), device_id_type=MESH,
            )
        )
        copies[-1].start()
    for k in range(n_group):
        mid[k] = partial[rows_of(k, q), :]
    for copy in copies:
        copy.wait()
    for k in range(n_group):
        total = mid[k]
        for d in range(1, n_sub):
            total += recv[d, k].astype(F32)
        mid[k] = total
    copies = []
    for d in range(1, n_group):
        other = lax.rem(g + d, n_group)
        copies.append(
            pltpu.make_async_remote_copy(
                src_ref=mid.at[other], dst_ref=recv_mid.at[d],
                send_sem=mid_send_sem.at[d], recv_sem=mid_recv_sem.at[d],
                device_id=(other, q), device_id_type=MESH,
            )
        )
        copies[-1].start()
    for copy in copies:
        copy.wait()
    total = mid[g]
    for d in range(1, n_group):
        total += recv_mid[d]
    out[...] = total


def on_device(
    n_group, n_sub,
    adjoint, velocity, face_speed, derivatives, lift_operator, emission_profile,
    neighbours, sub_sends, group_sends, element_tile, tile_slot,
):
    species, nodes, elements = adjoint.shape
    face_nodes = face_speed.shape[0] // FACES
    pad = padded_nodes(face_nodes)
    block = species * pad
    tiles = elements // SPAN
    cap = sub_sends.shape[1] // n_sub
    span_group = group_sends.shape[1]
    assert elements % SPAN == 0 and SPAN % (2 * cap) == 0 and 2 * cap == 128
    assert (n_sub * cap) % SPAN == 0 and span_group % SPAN == 0
    select = jnp.asarray(select_matrix(nodes), BF16)
    spread = jnp.asarray(spread_matrix(face_nodes), BF16)
    vmem = pl.BlockSpec(memory_space=pltpu.VMEM)
    dma = pltpu.SemaphoreType.DMA
    far_tiles = n_sub * cap // SPAN

    flux = pl.pallas_call(
        functools.partial(flux_kernel, n_group, n_sub, cap),
        out_shape=jax.ShapeDtypeStruct((species, FACES * pad, elements), BF16),
        in_specs=[pl.BlockSpec(memory_space=pl.ANY)] + [vmem] * 6,
        out_specs=vmem,
        scratch_shapes=[
            pltpu.VMEM((tiles, species, nodes, SPAN), F32),
            pltpu.VMEM((FACES, tiles * block, SPAN), BF16),
            pltpu.VMEM((FACES, block, elements), BF16),
            pltpu.VMEM((n_sub, 2, block, 2 * cap), BF16),
            pltpu.VMEM((n_sub, 2, block, 2 * cap), BF16),
            pltpu.VMEM((2, block, span_group), BF16),
            pltpu.VMEM((2, block, span_group), BF16),
            pltpu.VMEM((4, far_tiles * block, SPAN), BF16),
            dma((tiles,)), dma((n_sub,)), dma((n_sub,)), dma((2,)), dma((2,)),
        ],
        compiler_params=pltpu.CompilerParams(
            collective_id=0, has_side_effects=True, vmem_limit_bytes=56 * 2**20),
        name="flux",
    )(adjoint, face_speed, neighbours, sub_sends, group_sends, select, spread)

    tile_count = tile_slot.shape[0]
    heights = emission_profile.shape[1]
    whole = lambda shape: pl.BlockSpec(shape, lambda i: (0,) * len(shape))
    along = lambda *lead: pl.BlockSpec(lead + (SPAN,), lambda i: (0,) * len(lead) + (i,))
    slots = tile_slot.reshape(tile_count // 128, 128)
    adjoint_next, partial = pl.pallas_call(
        step_kernel,
        grid=(tiles,),
        out_shape=(
            jax.ShapeDtypeStruct(adjoint.shape, F32),
            jax.ShapeDtypeStruct((tile_count, species * heights), F32),
        ),
        in_specs=[
            along(species, nodes), along(velocity.shape[0], nodes), along(species, FACES * pad),
            whole(derivatives.shape), whole(lift_operator.shape), whole(emission_profile.shape),
            whole(spread.shape), along(1), whole(slots.shape),
        ],
        out_specs=(along(species, nodes), whole((tile_count, species * heights))),
        scratch_shapes=[pltpu.VMEM((nodes, FACES * pad), BF16)],
        compiler_params=pltpu.CompilerParams(vmem_limit_bytes=56 * 2**20),
        name="step",
    )(
        adjoint, velocity, flux, derivatives, lift_operator, emission_profile,
        spread, element_tile.reshape(1, elements), slots,
    )

    own = tile_count // (n_group * n_sub)
    width = species * heights
    emission_grad = pl.pallas_call(
        functools.partial(sum_kernel, n_group, n_sub),
        out_shape=jax.ShapeDtypeStruct((own, width), F32),
        in_specs=[vmem],
        out_specs=vmem,
        scratch_shapes=[
            pltpu.VMEM((n_sub, n_group, own, width), BF16),
            pltpu.VMEM((n_sub, n_group, own, width), BF16),
            pltpu.VMEM((n_group, own, width), F32),
            pltpu.VMEM((n_group, own, width), F32),
            dma((n_sub,)), dma((n_sub,)), dma((n_group,)), dma((n_group,)),
        ],
        compiler_params=pltpu.CompilerParams(
            collective_id=1, has_side_effects=True, vmem_limit_bytes=16 * 2**20),
        name="sum",
    )(partial)
    return adjoint_next, emission_grad


def solution(mesh):
    both = ("group", "sub")
    placed = (
        P(None, None, both), P(None, None, both), P(None, both), P(), P(), P(),
        P(None, both), P(None, both), P(None, both), P(both), P(),
    )
    return jax.shard_map(
        functools.partial(on_device, mesh.shape["group"], mesh.shape["sub"]),
        mesh=mesh,
        in_specs=placed,
        out_specs=(P(None, None, both), P(both, None)),
        check_vma=False,
    )
```

time: 456 us -> 62 us (0.14); the launches traced: 449 us -> 61.7 us
  local copies, waits for them, and re-layouts: 275 us -> 4.74 us
  other arithmetic: 59 us -> 0 us
  Pallas kernels: 0 us -> 56.3 us
  waiting for transfers between devices: 48.3 us -> 0 us
  matrix products: 42.5 us -> 0 us
  between operations: 15 us -> 0.65 us
  starting transfers between devices: 9.59 us -> 0 us
    gather x22 -> x0, local copies, waits for them, and re-layouts: 161 us -> none  [the longest x12 123 us: pool_take(): return jnp.take(pool_rows, positions, axis=2)]
    pallas_call x0 -> x3, Pallas kernels: none -> 56.3 us  [the longest x1 24.2 us: on_device(): pl.pallas_call(functools.partial(flux_kernel, n_group, n_sub, cap), out_s...]
    reduce_scatter x2 -> x0, waiting for transfers between devices: 48.2 us -> none  [the longest x1 26.5 us: on_device(): lax.psum_scatter(group_block, 'sub', scatter_dimension=0, tiled=True)]
    unnamed x51 -> x5, local copies, waits for them, and re-layouts: 48.5 us -> 4.74 us
    dot_general x3 -> x0, matrix products: 42.5 us -> none  [the longest x1 25.4 us: on_device(): jnp.einsum('dq,wqx->wdx', lift_operator, face_flux_values, preferred_elem...]
    concatenate x6 -> x0, local copies, waits for them, and re-layouts: 29 us -> none  [pool_take(): pool_rows = jnp.concatenate([local_traces, received_part], axis=2)]
    squeeze x7 -> x0, local copies, waits for them, and re-layouts: 23.6 us -> none  [the longest x3 12.7 us: on_device(): outside_list.append(pool_take(traces[:, trace_id], group_part, shifted))]
    concatenate x6 -> x0, other arithmetic: 12.6 us -> none  [pool_take(): pool_rows = jnp.concatenate([local_traces, received_part], axis=2)]
  transfers between devices with their start and end apart: 5 -> 0, of which waited for: 2 -> 0; matrix products, arithmetic and copies ran while one was open for 27% -> 0% of each run, Pallas kernels for 0% -> 0%
where the time goes in v1:
time: 62 us; the launch traced here: 61.7 us
  Pallas kernels  56.3 us (91%)
  local copies, waits for them, and re-layouts  4.74 us (8%)
  between operations  0.65 us (1%)
    pallas_call x1, Pallas kernels, on_device(): pl.pallas_call(functools.partial(flux_kernel, n_group, n_sub, cap), out_s...  24.2 us
    pallas_call x1, Pallas kernels, on_device(): pl.pallas_call(step_kernel, grid=(tiles,), out_shape=(jax.ShapeDtypeStruc...  18.6 us
    pallas_call x1, Pallas kernels, on_device(): pl.pallas_call(functools.partial(sum_kernel, n_group, n_sub), out_shape=j...  13.5 us
    unnamed x5, local copies, waits for them, and re-layouts  4.74 us

profile of v1, /device:TPU:0, one launch (start us, length us, event | category | flops | bytes accessed | tf_op | source)
XLA Modules:
  0.0 61.7 jit_solution(1552111461318641951)
XLA Ops:
  0.6 1.4 %copy.16.profile = bf16[256,32]{1,0:T(8,128)(2,1)} copy(bf16[256,32]{0,1:T(8,128)(2,1)} %param.18) | data formatting | bytes 32768 | tf_op args[5]
  2.1 1.6 %copy.15.lift = bf16[256,216]{1,0:T(8,128)(2,1)} copy(bf16[256,216]{0,1:T(8,128)(2,1)} %param.17) | data formatting | bytes 221184 | tf_op args[4]
  3.7 24.2 %flux.1 = bf16[4,240,2048]{2,1,0:T(8,128)(2,1)} custom-call(f32[4,256,2048]{2,1,0:T(8,128)} %adjoint.3, bf16[216,2048]{1,0:T(8,128)(2,1)} %speed.1, s32[6,2048]{1,0:T(8,128)} %neighbours.1, s32[4,512]{1,0:T(4,128)} %sub_sends.1, s32[2,256]{1,0:T(2,128)} %group_sends.1, bf16[240,256]{1,0:T(8,128)(2,1)} %constant.4.clone.select, ...), custom_call_target="tpu_custom_call" | custom-call | tf_op jit(solution)/shard_map/flux/pallas_call | solution.py:327
  27.9 18.6 %step.1 = (f32[4,256,2048]{2,1,0:T(8,128)}, f32[1024,128]{1,0:T(8,128)}) custom-call(f32[4,256,2048]{2,1,0:T(8,128)} %adjoint.3, bf16[3,256,2048]{2,1,0:T(8,128)(2,1)} %velocity.1, bf16[4,240,2048]{2,1,0:T(8,128)(2,1)} %flux.1, bf16[768,256]{1,0:T(8,128)(2,1)} %derivatives.1, bf16[256,216]{1,0:T(8,128)(2,1)} %copy.15.lift, bf16[256,32]{1,0:T(8,128)(2,1)} %copy.16.profile, ...), custom_call_target="tpu_custom_call" | custom-call | tf_op jit(solution)/shard_map/step/pallas_call | solution.py:353
  46.5 0.0 copy-start
  46.5 1.0 %copy-done = f32[1024,128]{1,0:T(8,128)S(1)} copy-done((f32[1024,128]{1,0:T(8,128)S(1)}, f32[1024,128]{1,0:T(8,128)}, u32[]{:S(2)}) %copy-start) | copy-done | bytes 524312
  47.5 13.5 %sum.1 = f32[32,128]{1,0:T(8,128)S(1)} custom-call(f32[1024,128]{1,0:T(8,128)S(1)} %copy-done), custom_call_target="tpu_custom_call" | custom-call | tf_op jit(solution)/shard_map/sum/pallas_call | solution.py:376
  61.1 0.6 copy.18
Async XLA Ops:
  46.5 1.0 %copy-start = (f32[1024,128]{1,0:T(8,128)S(1)}, f32[1024,128]{1,0:T(8,128)}, u32[]{:S(2)}) copy-start(f32[1024,128]{1,0:T(8,128)} %get-tuple-element.5.partial) | copy-start | bytes 1572868

commit v2 on v1

--- a/solution.py
+++ b/solution.py
@@ -12,6 +12,7 @@
 SECTION = 0.125
 FACES = 6
 SPAN = 256
+WIDE = 512
 MESH = pl.DeviceIdType.MESH
 F32, BF16 = jnp.float32, jnp.bfloat16
 
@@ -61,15 +62,15 @@
 
 
 def one_hot_rows(index, rows):
-    ids = lax.broadcasted_iota(jnp.int32, (rows, index.shape[1]), 0)
-    return jnp.where(ids == index, 1.0, 0.0).astype(BF16)
+    ids = lax.broadcasted_iota(jnp.int32, (rows, index.shape[1]), 0).astype(jnp.int16)
+    return jnp.where(ids == index.astype(jnp.int16), jnp.ones((), BF16), jnp.zeros((), BF16))
 
 
 def columns_of(stack, position, first, count, block):
     picked = dot(stack, one_hot_rows(position & (SPAN - 1), SPAN))
     tile = position >> (SPAN.bit_length() - 1)
-    out = jnp.zeros((block, position.shape[1]), F32)
-    for t in range(count):
+    out = picked[:block]
+    for t in range(1, count):
         out = jnp.where(tile == first + t, picked[t * block : (t + 1) * block], out)
     return out
 
@@ -102,28 +103,31 @@
         pl.semaphore_signal(barrier, inc=1, device_id=peer, device_id_type=MESH)
 
     def trace_tile(i, carry):
-        field_copy(i).wait()
-        parts = [dot(select[...], field[i, s].astype(BF16)) for s in range(species)]
-        rows = pl.ds(pl.multiple_of(i * block, block), block)
-        for f in range(FACES):
-            one = jnp.concatenate([p[f * pad : (f + 1) * pad] for p in parts], axis=0)
-            table[f, rows, :] = one.astype(BF16)
+        for j in range(WIDE // SPAN):
+            field_copy(i * (WIDE // SPAN) + j).wait()
+        for j in range(WIDE // SPAN):
+            tile = i * (WIDE // SPAN) + j
+            parts = [dot(select[...], field[tile, s].astype(BF16)) for s in range(species)]
+            rows = pl.ds(pl.multiple_of(tile * block, block), block)
+            for f in range(FACES):
+                one = jnp.concatenate([p[f * pad : (f + 1) * pad] for p in parts], axis=0)
+                table[f, rows, :] = one.astype(BF16)
         return carry
 
-    lax.fori_loop(0, tiles, trace_tile, 0)
+    lax.fori_loop(0, tiles * SPAN // WIDE, trace_tile, 0)
 
     low_half = lax.broadcasted_iota(jnp.int32, (block, 2 * cap), 1) < cap
     for axis_id in range(2):
-        for c in range(n_sub * cap // SPAN):
-            cols = slice(c * SPAN, (c + 1) * SPAN)
+        for c in range(n_sub * cap // WIDE):
+            cols = slice(c * WIDE, (c + 1) * WIDE)
             minus, plus = [
                 columns_of(table[f], sub_sends[f : f + 1, cols], 0, tiles, block)
                 for f in (2 * axis_id, 2 * axis_id + 1)
             ]
-            for m in range(SPAN // (2 * cap)):
+            for m in range(WIDE // (2 * cap)):
                 part = slice(m * 2 * cap, (m + 1) * 2 * cap)
                 a, b = minus[:, part], plus[:, part]
-                r = c * (SPAN // cap) + 2 * m
+                r = c * (WIDE // cap) + 2 * m
                 send_sub[r, axis_id] = jnp.where(low_half, a, pltpu.roll(b, cap, 1)).astype(BF16)
                 send_sub[r + 1, axis_id] = jnp.where(low_half, pltpu.roll(a, cap, 1), b).astype(BF16)
     pl.semaphore_wait(barrier, len(peers))
@@ -155,13 +159,13 @@
     recv_sub[q] = jnp.zeros(recv_sub.shape[1:], BF16)
 
     def local_tile(i, carry):
-        cols = pl.ds(pl.multiple_of(i * SPAN, SPAN), SPAN)
+        cols = pl.ds(pl.multiple_of(i * WIDE, WIDE), WIDE)
         for f in range(FACES):
             got = columns_of(table[f ^ 1], neighbours[f : f + 1, cols], 0, tiles, block)
             local[f, :, cols] = got.astype(BF16)
         return carry
 
-    lax.fori_loop(0, tiles, local_tile, 0)
+    lax.fori_loop(0, elements // WIDE, local_tile, 0)
 
     for copy in copies:
         copy.wait()
@@ -179,8 +183,8 @@
                     lane % SPAN : lane % SPAN + 2 * cap] = both.astype(BF16)
 
     def flux_tile(i, carry):
-        cols = pl.ds(pl.multiple_of(i * SPAN, SPAN), SPAN)
-        rows = pl.ds(pl.multiple_of(i * block, block), block)
+        cols = pl.ds(pl.multiple_of(i * WIDE, WIDE), WIDE)
+        inside = WIDE // SPAN
         upwind = jnp.maximum(dot(spread[...], speed[:, cols]), 0.0)
         parts = []
         for f in range(FACES):
@@ -189,19 +193,24 @@
             if t < 4:
                 far = columns_of(far_sub[t], position, tiles, far_tiles, block)
             else:
-                far = jnp.zeros((block, SPAN), F32)
-                for c in range(span_group // SPAN):
-                    got = recv_group[t - 4, :, c * SPAN : (c + 1) * SPAN]
-                    far += columns_of(got, position, tiles + far_tiles + c, 1, block)
-            outside = local[f, :, cols].astype(F32) + far
+                stack = jnp.concatenate([
+                    recv_group[t - 4, :, c * SPAN : (c + 1) * SPAN]
+                    for c in range(span_group // SPAN)
+                ], axis=0)
+                far = columns_of(stack, position, tiles + far_tiles, span_group // SPAN, block)
+            outside = jnp.where(position >= elements, far, local[f, :, cols].astype(F32))
             wind = jnp.concatenate([upwind[f * pad : (f + 1) * pad]] * species, axis=0)
-            parts.append(wind * (outside - table[f, rows, :].astype(F32)))
+            here = jnp.concatenate([
+                table[f, pl.ds(pl.multiple_of((i * inside + j) * block, block), block), :]
+                for j in range(inside)
+            ], axis=1)
+            parts.append(wind * (outside - here.astype(F32)))
         for s in range(species):
             one = jnp.concatenate([p[s * pad : (s + 1) * pad] for p in parts], axis=0)
             flux[s, :, cols] = one.astype(BF16)
         return carry
 
-    lax.fori_loop(0, tiles, flux_tile, 0)
+    lax.fori_loop(0, elements // WIDE, flux_tile, 0)
 
 
 def step_kernel(
@@ -213,7 +222,7 @@
 
     @pl.when(pl.program_id(0) == 0)
     def _():
-        lift_wide[...] = dot_nt(lift[...], spread[...]).astype(BF16)
+        lift_wide[...] = dot(spread[...], lift[...]).T.astype(BF16)
         partial[...] = jnp.zeros_like(partial)
 
     tile = element_tile[...]
@@ -226,16 +235,16 @@
     row = jnp.sum(jnp.where(which, picked, 0.0), axis=0, keepdims=True).astype(jnp.int32)
 
     contrib = []
+    wind = [velocity[d].astype(F32) for d in range(3)]
     for s in range(species):
         field = adjoint[s]
         grads = dot(derivatives[...], field.astype(BF16))
         total = dot(lift_wide[...], flux[s])
         for d in range(3):
-            total += velocity[d].astype(F32) * grads[d * nodes : (d + 1) * nodes]
+            total += wind[d] * grads[d * nodes : (d + 1) * nodes]
         result = field + SECTION * total
         adjoint_next[s] = result
-        contrib.append(lax.dot_general(
-            profile[...], result.astype(BF16), (((0,), (0,)), ((), ())), preferred_element_type=F32))
+        contrib.append(dot(profile[...], result.astype(BF16)))
     terms = jnp.concatenate(contrib, axis=0)
     first = terms.astype(BF16)
     second = (terms - first.astype(F32)).astype(BF16)
@@ -247,10 +256,12 @@
 
 def sum_kernel(
     n_group, n_sub,
-    partial, out,
-    send, recv, mid, recv_mid,
-    send_sem, recv_sem, mid_send_sem, mid_recv_sem,
+    partial_hbm, out,
+    partial, send, recv, mid, recv_mid,
+    load_sem, send_sem, recv_sem, mid_send_sem, mid_recv_sem,
 ):
+    load = pltpu.make_async_copy(partial_hbm, partial, load_sem)
+    load.start()
     own = out.shape[0]
     g, q = lax.axis_index("group"), lax.axis_index("sub")
     barrier = pltpu.get_barrier_semaphore()
@@ -262,6 +273,7 @@
     def rows_of(group, sub):
         return pl.ds(pl.multiple_of((group * n_sub + sub) * own, own), own)
 
+    load.wait()
     for d in range(1, n_sub):
         for k in range(n_group):
             send[d, k] = partial[rows_of(k, lax.rem(q + d, n_sub)), :].astype(BF16)
@@ -316,7 +328,7 @@
     tiles = elements // SPAN
     cap = sub_sends.shape[1] // n_sub
     span_group = group_sends.shape[1]
-    assert elements % SPAN == 0 and SPAN % (2 * cap) == 0 and 2 * cap == 128
+    assert elements % WIDE == 0 and n_sub * cap % WIDE == 0 and SPAN % (2 * cap) == 0 and 2 * cap == 128
     assert (n_sub * cap) % SPAN == 0 and span_group % SPAN == 0
     select = jnp.asarray(select_matrix(nodes), BF16)
     spread = jnp.asarray(spread_matrix(face_nodes), BF16)
@@ -348,18 +360,18 @@
     tile_count = tile_slot.shape[0]
     heights = emission_profile.shape[1]
     whole = lambda shape: pl.BlockSpec(shape, lambda i: (0,) * len(shape))
-    along = lambda *lead: pl.BlockSpec(lead + (SPAN,), lambda i: (0,) * len(lead) + (i,))
+    along = lambda *lead: pl.BlockSpec(lead + (WIDE,), lambda i: (0,) * len(lead) + (i,))
     slots = tile_slot.reshape(tile_count // 128, 128)
     adjoint_next, partial = pl.pallas_call(
         step_kernel,
-        grid=(tiles,),
+        grid=(elements // WIDE,),
         out_shape=(
             jax.ShapeDtypeStruct(adjoint.shape, F32),
             jax.ShapeDtypeStruct((tile_count, species * heights), F32),
         ),
         in_specs=[
             along(species, nodes), along(velocity.shape[0], nodes), along(species, FACES * pad),
-            whole(derivatives.shape), whole(lift_operator.shape), whole(emission_profile.shape),
+            whole(derivatives.shape), whole(lift_operator.shape[::-1]), whole(emission_profile.shape[::-1]),
             whole(spread.shape), along(1), whole(slots.shape),
         ],
         out_specs=(along(species, nodes), whole((tile_count, species * heights))),
@@ -367,7 +379,7 @@
         compiler_params=pltpu.CompilerParams(vmem_limit_bytes=56 * 2**20),
         name="step",
     )(
-        adjoint, velocity, flux, derivatives, lift_operator, emission_profile,
+        adjoint, velocity, flux, derivatives, lift_operator.T, emission_profile.T,
         spread, element_tile.reshape(1, elements), slots,
     )
 
@@ -376,17 +388,18 @@
     emission_grad = pl.pallas_call(
         functools.partial(sum_kernel, n_group, n_sub),
         out_shape=jax.ShapeDtypeStruct((own, width), F32),
-        in_specs=[vmem],
+        in_specs=[pl.BlockSpec(memory_space=pl.ANY)],
         out_specs=vmem,
         scratch_shapes=[
+            pltpu.VMEM((tile_count, width), F32),
             pltpu.VMEM((n_sub, n_group, own, width), BF16),
             pltpu.VMEM((n_sub, n_group, own, width), BF16),
             pltpu.VMEM((n_group, own, width), F32),
             pltpu.VMEM((n_group, own, width), F32),
-            dma((n_sub,)), dma((n_sub,)), dma((n_group,)), dma((n_group,)),
+            dma, dma((n_sub,)), dma((n_sub,)), dma((n_group,)), dma((n_group,)),
         ],
         compiler_params=pltpu.CompilerParams(
-            collective_id=1, has_side_effects=True, vmem_limit_bytes=16 * 2**20),
+            collective_id=1, has_side_effects=True, vmem_limit_bytes=56 * 2**20),
         name="sum",
     )(partial)
     return adjoint_next, emission_grad

time: 62 us -> 54.8 us (0.88)
  Pallas kernels: 56.3 us -> 52.5 us
  local copies, waits for them, and re-layouts: 4.74 us -> 1.32 us
    unnamed x5 -> x1, local copies, waits for them, and re-layouts: 4.74 us -> 1.32 us
    pallas_call x1, Pallas kernels: 18.6 us -> 15.7 us  [on_device(): pl.pallas_call(step_kernel, grid=(elements // WIDE,), out_shape=(jax.Shap...]
    pallas_call x1, Pallas kernels: 24.2 us -> 22.7 us  [on_device(): pl.pallas_call(functools.partial(flux_kernel, n_group, n_sub, cap), out_s...]
    pallas_call x1, Pallas kernels: 13.5 us -> 14.2 us  [on_device(): pl.pallas_call(functools.partial(sum_kernel, n_group, n_sub), out_shape=j...]
where the time goes in v2:
time: 54.8 us; the launch traced here: 54.5 us
  Pallas kernels  52.5 us (96%)
  local copies, waits for them, and re-layouts  1.32 us (2%)
  between operations  0.65 us (1%)
    pallas_call x1, Pallas kernels, on_device(): pl.pallas_call(functools.partial(flux_kernel, n_group, n_sub, cap), out_s...  22.7 us
    pallas_call x1, Pallas kernels, on_device(): pl.pallas_call(step_kernel, grid=(elements // WIDE,), out_shape=(jax.Shap...  15.7 us
    pallas_call x1, Pallas kernels, on_device(): pl.pallas_call(functools.partial(sum_kernel, n_group, n_sub), out_shape=j...  14.2 us
    unnamed x1, local copies, waits for them, and re-layouts  1.32 us

profile of v2, /device:TPU:0, one launch (start us, length us, event | category | flops | bytes accessed | tf_op | source)
XLA Modules:
  0.0 54.5 jit_solution(17388561212010957270)
XLA Ops:
  0.6 22.7 %flux.1 = bf16[4,240,2048]{2,1,0:T(8,128)(2,1)} custom-call(f32[4,256,2048]{2,1,0:T(8,128)} %adjoint.3, bf16[216,2048]{1,0:T(8,128)(2,1)} %speed.1, s32[6,2048]{1,0:T(8,128)} %neighbours.1, s32[4,512]{1,0:T(4,128)} %sub_sends.1, s32[2,256]{1,0:T(2,128)} %group_sends.1, bf16[240,256]{1,0:T(8,128)(2,1)} %constant.4.clone.select, ...), custom_call_target="tpu_custom_call" | custom-call | tf_op jit(solution)/shard_map/flux/pallas_call | solution.py:339
  23.4 15.7 %step.1 = (f32[4,256,2048]{2,1,0:T(8,128)}, f32[1024,128]{1,0:T(8,128)}) custom-call(f32[4,256,2048]{2,1,0:T(8,128)} %adjoint.3, bf16[3,256,2048]{2,1,0:T(8,128)(2,1)} %velocity.1, bf16[4,240,2048]{2,1,0:T(8,128)(2,1)} %flux.1, bf16[768,256]{1,0:T(8,128)(2,1)} %derivatives.1, bf16[216,256]{1,0:T(8,128)(2,1)} %bitcast.4, bf16[32,256]{1,0:T(8,128)(2,1)} %bitcast.5, ...), custom_call_target="tpu_custom_call" | custom-call | tf_op jit(solution)/shard_map/step/pallas_call | solution.py:365
  39.0 14.2 %sum.1 = f32[32,128]{1,0:T(8,128)} custom-call(f32[1024,128]{1,0:T(8,128)} %get-tuple-element.5.partial_hbm), custom_call_target="tpu_custom_call" | custom-call | tf_op jit(solution)/shard_map/sum/pallas_call | solution.py:388
  53.2 1.3 %copy.16 = f32[32,128]{1,0:T(8,128)} copy(f32[32,128]{1,0:T(8,128)} %sum.1) | data formatting | bytes 32768

commit v3 on v2

--- a/solution.py
+++ b/solution.py
@@ -13,6 +13,7 @@
 FACES = 6
 SPAN = 256
 WIDE = 512
+STRIP = 16
 MESH = pl.DeviceIdType.MESH
 F32, BF16 = jnp.float32, jnp.bfloat16
 
@@ -66,13 +67,14 @@
     return jnp.where(ids == index.astype(jnp.int16), jnp.ones((), BF16), jnp.zeros((), BF16))
 
 
-def columns_of(stack, position, first, count, block):
-    picked = dot(stack, one_hot_rows(position & (SPAN - 1), SPAN))
-    tile = position >> (SPAN.bit_length() - 1)
-    out = picked[:block]
-    for t in range(1, count):
-        out = jnp.where(tile == first + t, picked[t * block : (t + 1) * block], out)
-    return out
+def columns_of(stack, position, first, count, block, picked, emit):
+    picked[: count * block, :] = dot(stack, one_hot_rows(position & (SPAN - 1), SPAN))
+    tile = jnp.broadcast_to(position >> (SPAN.bit_length() - 1), (STRIP, position.shape[1]))
+    for r in range(0, block, STRIP):
+        rows = picked[r : r + STRIP, :]
+        for t in range(1, count):
+            rows = jnp.where(tile == first + t, picked[t * block + r : t * block + r + STRIP, :], rows)
+        emit(r, rows)
 
 
 def flux_kernel(
@@ -80,7 +82,8 @@
     adjoint, speed, neighbours, sub_sends, group_sends, select, spread,
     flux,
     field, table, local, send_sub, recv_sub, send_group, recv_group, far_sub,
-    field_sem, sub_send_sem, sub_recv_sem, group_send_sem, group_recv_sem,
+    picked, upwind, flux_wide, flux_out,
+    field_sem, flux_sem, sub_send_sem, sub_recv_sem, group_send_sem, group_recv_sem,
 ):
     tiles, species = field.shape[0], field.shape[1]
     pad = select.shape[0] // FACES
@@ -116,20 +119,27 @@
 
     lax.fori_loop(0, tiles * SPAN // WIDE, trace_tile, 0)
 
-    low_half = lax.broadcasted_iota(jnp.int32, (block, 2 * cap), 1) < cap
+    low_half = lax.broadcasted_iota(jnp.int32, (STRIP, 2 * cap), 1) < cap
     for axis_id in range(2):
         for c in range(n_sub * cap // WIDE):
             cols = slice(c * WIDE, (c + 1) * WIDE)
-            minus, plus = [
-                columns_of(table[f], sub_sends[f : f + 1, cols], 0, tiles, block)
-                for f in (2 * axis_id, 2 * axis_id + 1)
-            ]
-            for m in range(WIDE // (2 * cap)):
-                part = slice(m * 2 * cap, (m + 1) * 2 * cap)
-                a, b = minus[:, part], plus[:, part]
-                r = c * (WIDE // cap) + 2 * m
-                send_sub[r, axis_id] = jnp.where(low_half, a, pltpu.roll(b, cap, 1)).astype(BF16)
-                send_sub[r + 1, axis_id] = jnp.where(low_half, pltpu.roll(a, cap, 1), b).astype(BF16)
+            def keep(r, rows):
+                flux_wide[0, r : r + STRIP, :] = rows
+
+            def merge(r, plus):
+                minus = flux_wide[0, r : r + STRIP, :]
+                for m in range(WIDE // (2 * cap)):
+                    part = slice(m * 2 * cap, (m + 1) * 2 * cap)
+                    a, b = minus[:, part], plus[:, part]
+                    to = c * (WIDE // cap) + 2 * m
+                    send_sub[to, axis_id, r : r + STRIP, :] = jnp.where(
+                        low_half, a, pltpu.roll(b, cap, 1)).astype(BF16)
+                    send_sub[to + 1, axis_id, r : r + STRIP, :] = jnp.where(
+                        low_half, pltpu.roll(a, cap, 1), b).astype(BF16)
+
+            for k, emit in ((0, keep), (1, merge)):
+                f = 2 * axis_id + k
+                columns_of(table[f], sub_sends[f : f + 1, cols], 0, tiles, block, picked.at[k], emit)
     pl.semaphore_wait(barrier, len(peers))
     copies = []
     for d in range(1, n_sub):
@@ -146,8 +156,13 @@
     for k, target in ((0, below), (1, above)):
         for c in range(span_group // SPAN):
             cols = slice(c * SPAN, (c + 1) * SPAN)
-            got = columns_of(table[4 + k], group_sends[k : k + 1, cols], 0, tiles, block)
-            send_group[k, :, cols] = got.astype(BF16)
+
+            def keep(r, rows):
+                send_group[k, r : r + STRIP, cols] = rows.astype(BF16)
+
+            columns_of(
+                table[4 + k], group_sends[k : k + 1, cols], 0, tiles, block,
+                picked.at[k, :, :SPAN], keep)
         copies.append(
             pltpu.make_async_remote_copy(
                 src_ref=send_group.at[k], dst_ref=recv_group.at[k],
@@ -161,8 +176,12 @@
     def local_tile(i, carry):
         cols = pl.ds(pl.multiple_of(i * WIDE, WIDE), WIDE)
         for f in range(FACES):
-            got = columns_of(table[f ^ 1], neighbours[f : f + 1, cols], 0, tiles, block)
-            local[f, :, cols] = got.astype(BF16)
+
+            def keep(r, rows):
+                local[f, r : r + STRIP, cols] = rows.astype(BF16)
+
+            columns_of(
+                table[f ^ 1], neighbours[f : f + 1, cols], 0, tiles, block, picked.at[f % 2], keep)
         return carry
 
     lax.fori_loop(0, elements // WIDE, local_tile, 0)
@@ -172,50 +191,64 @@
     far_tiles = n_sub * cap // SPAN
     for t in range(4):
         for r in range(0, n_sub, 2):
-            a = recv_sub[r, t // 2].astype(F32)
-            b = recv_sub[r + 1, t // 2].astype(F32)
-            if t % 2 == 0:
-                both = jnp.where(low_half, a, pltpu.roll(b, cap, 1))
-            else:
-                both = jnp.where(low_half, pltpu.roll(a, cap, 1), b)
             lane = r * cap
-            far_sub[t, (lane // SPAN) * block : (lane // SPAN + 1) * block,
-                    lane % SPAN : lane % SPAN + 2 * cap] = both.astype(BF16)
+            for k in range(0, block, STRIP):
+                a = recv_sub[r, t // 2, k : k + STRIP, :].astype(F32)
+                b = recv_sub[r + 1, t // 2, k : k + STRIP, :].astype(F32)
+                if t % 2 == 0:
+                    both = jnp.where(low_half, a, pltpu.roll(b, cap, 1))
+                else:
+                    both = jnp.where(low_half, pltpu.roll(a, cap, 1), b)
+                row = (lane // SPAN) * block + k
+                far_sub[t, row : row + STRIP, lane % SPAN : lane % SPAN + 2 * cap] = both.astype(BF16)
+
+    def flux_copy(i):
+        cols = pl.ds(pl.multiple_of(i * WIDE, WIDE), WIDE)
+        return pltpu.make_async_copy(flux_out.at[i], flux.at[:, :, cols], flux_sem.at[i])
 
     def flux_tile(i, carry):
         cols = pl.ds(pl.multiple_of(i * WIDE, WIDE), WIDE)
         inside = WIDE // SPAN
-        upwind = jnp.maximum(dot(spread[...], speed[:, cols]), 0.0)
-        parts = []
+        upwind[...] = jnp.maximum(dot(spread[...], speed[:, cols]), 0.0)
         for f in range(FACES):
             t = f ^ 1
             position = neighbours[f : f + 1, cols]
+            remote = jnp.broadcast_to(position, (STRIP, WIDE)) >= elements
+
+            def keep(r, far):
+                outside = jnp.where(remote, far, local[f, r : r + STRIP, cols].astype(F32))
+                here = jnp.concatenate([
+                    table[f, pl.ds(pl.multiple_of((i * inside + j) * block + r, STRIP), STRIP), :]
+                    for j in range(inside)
+                ], axis=1)
+                jump = outside - here.astype(F32)
+                for h in range(0, STRIP, 8):
+                    s, k = (r + h) // pad, (r + h) % pad
+                    row = f * pad + k
+                    flux_wide[s, row : row + 8, :] = upwind[row : row + 8, :] * jump[h : h + 8]
+
             if t < 4:
-                far = columns_of(far_sub[t], position, tiles, far_tiles, block)
+                stack, first, count = far_sub[t], tiles, far_tiles
             else:
+                first, count = tiles + far_tiles, span_group // SPAN
                 stack = jnp.concatenate([
-                    recv_group[t - 4, :, c * SPAN : (c + 1) * SPAN]
-                    for c in range(span_group // SPAN)
+                    recv_group[t - 4, :, c * SPAN : (c + 1) * SPAN] for c in range(count)
                 ], axis=0)
-                far = columns_of(stack, position, tiles + far_tiles, span_group // SPAN, block)
-            outside = jnp.where(position >= elements, far, local[f, :, cols].astype(F32))
-            wind = jnp.concatenate([upwind[f * pad : (f + 1) * pad]] * species, axis=0)
-            here = jnp.concatenate([
-                table[f, pl.ds(pl.multiple_of((i * inside + j) * block, block), block), :]
-                for j in range(inside)
-            ], axis=1)
-            parts.append(wind * (outside - here.astype(F32)))
+            columns_of(stack, position, first, count, block, picked.at[f % 2], keep)
         for s in range(species):
-            one = jnp.concatenate([p[s * pad : (s + 1) * pad] for p in parts], axis=0)
-            flux[s, :, cols] = one.astype(BF16)
+            for r in range(0, FACES * pad, STRIP):
+                flux_out[i, s, r : r + STRIP, :] = flux_wide[s, r : r + STRIP, :].astype(BF16)
+        flux_copy(i).start()
         return carry
 
     lax.fori_loop(0, elements // WIDE, flux_tile, 0)
+    for i in range(elements // WIDE):
+        flux_copy(i).wait()
 
 
 def step_kernel(
     adjoint, velocity, flux, derivatives, lift, profile, spread, element_tile, tile_slot,
-    adjoint_next, partial, lift_wide,
+    adjoint_next, partial, lift_wide, grads, lifted, next_low,
 ):
     species, nodes, span = adjoint.shape
     tile_rows = partial.shape[0]
@@ -235,16 +268,20 @@
     row = jnp.sum(jnp.where(which, picked, 0.0), axis=0, keepdims=True).astype(jnp.int32)
 
     contrib = []
-    wind = [velocity[d].astype(F32) for d in range(3)]
     for s in range(species):
-        field = adjoint[s]
-        grads = dot(derivatives[...], field.astype(BF16))
-        total = dot(lift_wide[...], flux[s])
-        for d in range(3):
-            total += wind[d] * grads[d * nodes : (d + 1) * nodes]
-        result = field + SECTION * total
-        adjoint_next[s] = result
-        contrib.append(dot(profile[...], result.astype(BF16)))
+        slot = s % 2
+        grads[slot] = dot(derivatives[...], adjoint[s].astype(BF16))
+        lifted[slot] = dot(lift_wide[...], flux[s])
+        for r in range(0, nodes, STRIP):
+            rows = slice(r, r + STRIP)
+            total = lifted[slot, rows, :]
+            for d in range(3):
+                wind = velocity[d, rows, :].astype(F32)
+                total += wind * grads[slot, d * nodes + r : d * nodes + r + STRIP, :]
+            result = adjoint[s, rows, :] + SECTION * total
+            adjoint_next[s, rows, :] = result
+            next_low[slot, rows, :] = result.astype(BF16)
+        contrib.append(dot(profile[...], next_low[slot]))
     terms = jnp.concatenate(contrib, axis=0)
     first = terms.astype(BF16)
     second = (terms - first.astype(F32)).astype(BF16)
@@ -274,46 +311,45 @@
         return pl.ds(pl.multiple_of((group * n_sub + sub) * own, own), own)
 
     load.wait()
-    for d in range(1, n_sub):
-        for k in range(n_group):
-            send[d, k] = partial[rows_of(k, lax.rem(q + d, n_sub)), :].astype(BF16)
+    order = sorted(range(1, n_group), key=lambda d: -min(d, n_group - d)) + [0]
+    for e, step in enumerate(order):
+        k = lax.rem(g + step, n_group)
+        for d in range(1, n_sub):
+            send[e, d] = partial[rows_of(k, lax.rem(q + d, n_sub)), :].astype(BF16)
     pl.semaphore_wait(barrier, len(peers))
-    copies = []
-    for d in range(1, n_sub):
-        copies.append(
-            pltpu.make_async_remote_copy(
-                src_ref=send.at[d], dst_ref=recv.at[d],
-                send_sem=send_sem.at[d], recv_sem=recv_sem.at[d],
+    first = []
+    for e in range(n_group):
+        for d in range(1, n_sub):
+            copy = pltpu.make_async_remote_copy(
+                src_ref=send.at[e, d], dst_ref=recv.at[e, d],
+                send_sem=send_sem.at[e, d], recv_sem=recv_sem.at[e, d],
                 device_id=(g, lax.rem(q + d, n_sub)), device_id_type=MESH,
             )
+            copy.start()
+            first.append(copy)
+    second = []
+    for e, step in enumerate(order):
+        k = lax.rem(g + step, n_group)
+        total = partial[rows_of(k, q), :]
+        for d in range(1, n_sub):
+            first[e * (n_sub - 1) + d - 1].wait_recv()
+            total += recv[e, d].astype(F32)
+        if step == 0:
+            break
+        mid[e] = total
+        copy = pltpu.make_async_remote_copy(
+            src_ref=mid.at[e], dst_ref=recv_mid.at[e],
+            send_sem=mid_send_sem.at[e], recv_sem=mid_recv_sem.at[e],
+            device_id=(k, q), device_id_type=MESH,
         )
-        copies[-1].start()
-    for k in range(n_group):
-        mid[k] = partial[rows_of(k, q), :]
-    for copy in copies:
-        copy.wait()
-    for k in range(n_group):
-        total = mid[k]
-        for d in range(1, n_sub):
-            total += recv[d, k].astype(F32)
-        mid[k] = total
-    copies = []
-    for d in range(1, n_group):
-        other = lax.rem(g + d, n_group)
-        copies.append(
-            pltpu.make_async_remote_copy(
-                src_ref=mid.at[other], dst_ref=recv_mid.at[d],
-                send_sem=mid_send_sem.at[d], recv_sem=mid_recv_sem.at[d],
-                device_id=(other, q), device_id_type=MESH,
-            )
-        )
-        copies[-1].start()
-    for copy in copies:
-        copy.wait()
-    total = mid[g]
-    for d in range(1, n_group):
-        total += recv_mid[d]
+        copy.start()
+        second.append(copy)
+    for e, copy in enumerate(second):
+        copy.wait_recv()
+        total += recv_mid[e]
     out[...] = total
+    for copy in first + second:
+        copy.wait_send()
 
 
 def on_device(
@@ -340,7 +376,7 @@
         functools.partial(flux_kernel, n_group, n_sub, cap),
         out_shape=jax.ShapeDtypeStruct((species, FACES * pad, elements), BF16),
         in_specs=[pl.BlockSpec(memory_space=pl.ANY)] + [vmem] * 6,
-        out_specs=vmem,
+        out_specs=pl.BlockSpec(memory_space=pl.ANY),
         scratch_shapes=[
             pltpu.VMEM((tiles, species, nodes, SPAN), F32),
             pltpu.VMEM((FACES, tiles * block, SPAN), BF16),
@@ -350,7 +386,12 @@
             pltpu.VMEM((2, block, span_group), BF16),
             pltpu.VMEM((2, block, span_group), BF16),
             pltpu.VMEM((4, far_tiles * block, SPAN), BF16),
-            dma((tiles,)), dma((n_sub,)), dma((n_sub,)), dma((2,)), dma((2,)),
+            pltpu.VMEM((2, max(tiles, far_tiles) * block, WIDE), F32),
+            pltpu.VMEM((FACES * pad, WIDE), F32),
+            pltpu.VMEM((species, FACES * pad, WIDE), F32),
+            pltpu.VMEM((elements // WIDE, species, FACES * pad, WIDE), BF16),
+            dma((tiles,)), dma((elements // WIDE,)),
+            dma((n_sub,)), dma((n_sub,)), dma((2,)), dma((2,)),
         ],
         compiler_params=pltpu.CompilerParams(
             collective_id=0, has_side_effects=True, vmem_limit_bytes=56 * 2**20),
@@ -375,7 +416,12 @@
             whole(spread.shape), along(1), whole(slots.shape),
         ],
         out_specs=(along(species, nodes), whole((tile_count, species * heights))),
-        scratch_shapes=[pltpu.VMEM((nodes, FACES * pad), BF16)],
+        scratch_shapes=[
+            pltpu.VMEM((nodes, FACES * pad), BF16),
+            pltpu.VMEM((2, 3 * nodes, WIDE), F32),
+            pltpu.VMEM((2, nodes, WIDE), F32),
+            pltpu.VMEM((2, nodes, WIDE), BF16),
+        ],
         compiler_params=pltpu.CompilerParams(vmem_limit_bytes=56 * 2**20),
         name="step",
     )(
@@ -392,11 +438,11 @@
         out_specs=vmem,
         scratch_shapes=[
             pltpu.VMEM((tile_count, width), F32),
-            pltpu.VMEM((n_sub, n_group, own, width), BF16),
-            pltpu.VMEM((n_sub, n_group, own, width), BF16),
+            pltpu.VMEM((n_group, n_sub, own, width), BF16),
+            pltpu.VMEM((n_group, n_sub, own, width), BF16),
             pltpu.VMEM((n_group, own, width), F32),
             pltpu.VMEM((n_group, own, width), F32),
-            dma, dma((n_sub,)), dma((n_sub,)), dma((n_group,)), dma((n_group,)),
+            dma, dma((n_group, n_sub)), dma((n_group, n_sub)), dma((n_group,)), dma((n_group,)),
         ],
         compiler_params=pltpu.CompilerParams(
             collective_id=1, has_side_effects=True, vmem_limit_bytes=56 * 2**20),

time: 54.8 us -> 55.9 us (1.020)
  Pallas kernels: 52.5 us -> 53.7 us
    pallas_call x1, Pallas kernels: 22.7 us -> 24 us  [on_device(): pl.pallas_call(functools.partial(flux_kernel, n_group, n_sub, cap), out_s...]
where the time goes in v3:
time: 55.9 us; the launch traced here: 55.7 us
  Pallas kernels  53.7 us (96%)
  local copies, waits for them, and re-layouts  1.32 us (2%)
  between operations  0.65 us (1%)
    pallas_call x1, Pallas kernels, on_device(): pl.pallas_call(functools.partial(flux_kernel, n_group, n_sub, cap), out_s...  24 us
    pallas_call x1, Pallas kernels, on_device(): pl.pallas_call(step_kernel, grid=(elements // WIDE,), out_shape=(jax.Shap...  15.5 us
    pallas_call x1, Pallas kernels, on_device(): pl.pallas_call(functools.partial(sum_kernel, n_group, n_sub), out_shape=j...  14.2 us
    unnamed x1, local copies, waits for them, and re-layouts  1.32 us

profile of v3, /device:TPU:0, one launch (start us, length us, event | category | flops | bytes accessed | tf_op | source)
XLA Modules:
  0.0 55.7 jit_solution(13785851957532048758)
XLA Ops:
  0.6 24.0 %flux.1 = bf16[4,240,2048]{2,1,0:T(8,128)(2,1)} custom-call(f32[4,256,2048]{2,1,0:T(8,128)} %adjoint.3, bf16[216,2048]{1,0:T(8,128)(2,1)} %speed.1, s32[6,2048]{1,0:T(8,128)} %neighbours.1, s32[4,512]{1,0:T(4,128)} %sub_sends.1, s32[2,256]{1,0:T(2,128)} %group_sends.1, bf16[240,256]{1,0:T(8,128)(2,1)} %constant.4.clone.select, ...), custom_call_target="tpu_custom_call" | custom-call | tf_op jit(solution)/shard_map/flux/pallas_call | solution.py:375
  24.6 15.5 %step.1 = (f32[4,256,2048]{2,1,0:T(8,128)}, f32[1024,128]{1,0:T(8,128)}) custom-call(f32[4,256,2048]{2,1,0:T(8,128)} %adjoint.3, bf16[3,256,2048]{2,1,0:T(8,128)(2,1)} %velocity.1, bf16[4,240,2048]{2,1,0:T(8,128)(2,1)} %flux.1, bf16[768,256]{1,0:T(8,128)(2,1)} %derivatives.1, bf16[216,256]{1,0:T(8,128)(2,1)} %bitcast.4, bf16[32,256]{1,0:T(8,128)(2,1)} %bitcast.5, ...), custom_call_target="tpu_custom_call" | custom-call | tf_op jit(solution)/shard_map/step/pallas_call | solution.py:406
  40.2 14.2 %sum.1 = f32[32,128]{1,0:T(8,128)} custom-call(f32[1024,128]{1,0:T(8,128)} %get-tuple-element.5.partial_hbm), custom_call_target="tpu_custom_call" | custom-call | tf_op jit(solution)/shard_map/sum/pallas_call | solution.py:434
  54.3 1.3 %copy.16 = f32[32,128]{1,0:T(8,128)} copy(f32[32,128]{1,0:T(8,128)} %sum.1) | data formatting | bytes 32768

commit v4 on v2

--- a/solution.py
+++ b/solution.py
@@ -256,12 +256,10 @@
 
 def sum_kernel(
     n_group, n_sub,
-    partial_hbm, out,
-    partial, send, recv, mid, recv_mid,
-    load_sem, send_sem, recv_sem, mid_send_sem, mid_recv_sem,
+    partial, out,
+    send, recv, mid, recv_mid,
+    send_sem, recv_sem, mid_send_sem, mid_recv_sem,
 ):
-    load = pltpu.make_async_copy(partial_hbm, partial, load_sem)
-    load.start()
     own = out.shape[0]
     g, q = lax.axis_index("group"), lax.axis_index("sub")
     barrier = pltpu.get_barrier_semaphore()
@@ -273,7 +271,6 @@
     def rows_of(group, sub):
         return pl.ds(pl.multiple_of((group * n_sub + sub) * own, own), own)
 
-    load.wait()
     for d in range(1, n_sub):
         for k in range(n_group):
             send[d, k] = partial[rows_of(k, lax.rem(q + d, n_sub)), :].astype(BF16)
@@ -339,7 +336,7 @@
     flux = pl.pallas_call(
         functools.partial(flux_kernel, n_group, n_sub, cap),
         out_shape=jax.ShapeDtypeStruct((species, FACES * pad, elements), BF16),
-        in_specs=[pl.BlockSpec(memory_space=pl.ANY)] + [vmem] * 6,
+        in_specs=[pl.BlockSpec(memory_space=pltpu.HBM)] + [vmem] * 6,
         out_specs=vmem,
         scratch_shapes=[
             pltpu.VMEM((tiles, species, nodes, SPAN), F32),
@@ -353,7 +350,7 @@
             dma((tiles,)), dma((n_sub,)), dma((n_sub,)), dma((2,)), dma((2,)),
         ],
         compiler_params=pltpu.CompilerParams(
-            collective_id=0, has_side_effects=True, vmem_limit_bytes=56 * 2**20),
+            collective_id=0, has_side_effects=True, vmem_limit_bytes=46 * 2**20),
         name="flux",
     )(adjoint, face_speed, neighbours, sub_sends, group_sends, select, spread)
 
@@ -376,7 +373,7 @@
         ],
         out_specs=(along(species, nodes), whole((tile_count, species * heights))),
         scratch_shapes=[pltpu.VMEM((nodes, FACES * pad), BF16)],
-        compiler_params=pltpu.CompilerParams(vmem_limit_bytes=56 * 2**20),
+        compiler_params=pltpu.CompilerParams(vmem_limit_bytes=24 * 2**20),
         name="step",
     )(
         adjoint, velocity, flux, derivatives, lift_operator.T, emission_profile.T,
@@ -388,18 +385,17 @@
     emission_grad = pl.pallas_call(
         functools.partial(sum_kernel, n_group, n_sub),
         out_shape=jax.ShapeDtypeStruct((own, width), F32),
-        in_specs=[pl.BlockSpec(memory_space=pl.ANY)],
+        in_specs=[vmem],
         out_specs=vmem,
         scratch_shapes=[
-            pltpu.VMEM((tile_count, width), F32),
             pltpu.VMEM((n_sub, n_group, own, width), BF16),
             pltpu.VMEM((n_sub, n_group, own, width), BF16),
             pltpu.VMEM((n_group, own, width), F32),
             pltpu.VMEM((n_group, own, width), F32),
-            dma, dma((n_sub,)), dma((n_sub,)), dma((n_group,)), dma((n_group,)),
+            dma((n_sub,)), dma((n_sub,)), dma((n_group,)), dma((n_group,)),
         ],
         compiler_params=pltpu.CompilerParams(
-            collective_id=1, has_side_effects=True, vmem_limit_bytes=56 * 2**20),
+            collective_id=1, has_side_effects=True, vmem_limit_bytes=16 * 2**20),
         name="sum",
     )(partial)
     return adjoint_next, emission_grad

time: 54.8 us -> 55.4 us (1.011)
  local copies, waits for them, and re-layouts: 1.32 us -> 7.27 us
  Pallas kernels: 52.5 us -> 47.1 us
    unnamed x1 -> x27, local copies, waits for them, and re-layouts: 1.32 us -> 7.27 us
    pallas_call x1, Pallas kernels: 22.7 us -> 19.7 us  [on_device(): pl.pallas_call(functools.partial(flux_kernel, n_group, n_sub, cap), out_s...]
    pallas_call x1, Pallas kernels: 15.7 us -> 14 us  [on_device(): pl.pallas_call(step_kernel, grid=(elements // WIDE,), out_shape=(jax.Shap...]
    pallas_call x1, Pallas kernels: 14.2 us -> 13.5 us  [on_device(): pl.pallas_call(functools.partial(sum_kernel, n_group, n_sub), out_shape=j...]
where the time goes in v4:
time: 55.4 us; the launch traced here: 55.1 us
  Pallas kernels  47.1 us (85%)
  local copies, waits for them, and re-layouts  7.27 us (13%)
  between operations  0.75 us (1%)
    pallas_call x1, Pallas kernels, on_device(): pl.pallas_call(functools.partial(flux_kernel, n_group, n_sub, cap), out_s...  19.7 us
    pallas_call x1, Pallas kernels, on_device(): pl.pallas_call(step_kernel, grid=(elements // WIDE,), out_shape=(jax.Shap...  14 us
    pallas_call x1, Pallas kernels, on_device(): pl.pallas_call(functools.partial(sum_kernel, n_group, n_sub), out_shape=j...  13.5 us
    unnamed x27, local copies, waits for them, and re-layouts  7.27 us

profile of v4, /device:TPU:0, one launch (start us, length us, event | category | flops | bytes accessed | tf_op | source)
XLA Modules:
  0.0 55.1 jit_solution(12109625918790535984)
XLA Ops:
  0.6 0.0 copy-start
  0.6 0.0 copy-start.1
  0.7 0.0 copy-start.2
  0.7 1.3 %copy-done.2 = bf16[216,2048]{1,0:T(8,128)(2,1)S(1)} copy-done((bf16[216,2048]{1,0:T(8,128)(2,1)S(1)}, bf16[216,2048]{1,0:T(8,128)(2,1)}, u32[]{:S(2)}) %copy-start.2) | copy-done | bytes 884760
  2.0 0.0 copy-start.3
  2.0 1.5 %copy-done.3 = bf16[240,216]{1,0:T(8,128)(2,1)S(1)} copy-done((bf16[240,216]{1,0:T(8,128)(2,1)S(1)}, bf16[240,216]{1,0:T(8,128)(2,1)}, u32[]{:S(2)}) %copy-start.3) | copy-done | bytes 103704
  3.4 0.0 copy-start.5
  3.4 1.6 %copy-done.5 = bf16[240,256]{1,0:T(8,128)(2,1)S(1)} copy-done((bf16[240,256]{1,0:T(8,128)(2,1)S(1)}, bf16[240,256]{1,0:T(8,128)(2,1)}, u32[]{:S(2)}) %copy-start.5) | copy-done | bytes 122904
  5.1 0.0 copy-start.7
  5.1 0.8 %copy-done.7 = s32[6,2048]{1,0:T(8,128)S(1)} copy-done((s32[6,2048]{1,0:T(8,128)S(1)}, s32[6,2048]{1,0:T(8,128)}, u32[]{:S(2)}) %copy-start.7) | copy-done | bytes 49176
  5.9 0.0 copy-start.9
  5.9 0.7 %copy-done.9 = s32[4,512]{1,0:T(4,128)S(1)} copy-done((s32[4,512]{1,0:T(4,128)S(1)}, s32[4,512]{1,0:T(4,128)}, u32[]{:S(2)}) %copy-start.9) | copy-done | bytes 8216
  6.6 0.0 copy-start.12
  6.6 0.7 %copy-done.12 = s32[2,256]{1,0:T(2,128)S(1)} copy-done((s32[2,256]{1,0:T(2,128)S(1)}, s32[2,256]{1,0:T(2,128)}, u32[]{:S(2)}) %copy-start.12) | copy-done | bytes 2072
  7.3 0.0 copy-start.4
  7.3 0.0 copy-start.6
  7.3 0.0 copy-start.8
  7.3 0.0 copy-start.10
  7.3 0.0 copy-start.11
  7.3 19.7 %flux.1 = bf16[4,240,2048]{2,1,0:T(8,128)(2,1)S(1)} custom-call(f32[4,256,2048]{2,1,0:T(8,128)} %adjoint.3, bf16[216,2048]{1,0:T(8,128)(2,1)S(1)} %copy-done.2, s32[6,2048]{1,0:T(8,128)S(1)} %copy-done.7, s32[4,512]{1,0:T(4,128)S(1)} %copy-done.9, s32[2,256]{1,0:T(2,128)S(1)} %copy-done.12, bf16[240,256]{1,0:T(8,128)(2,1)S(1)} %copy-done.5, ...), custom_call_target="tpu_custom_call" | custom-call | tf_op jit(solution)/shard_map/flux/pallas_call | solution.py:336
  27.0 0.0 copy-done
  27.0 0.0 copy-done.1
  27.0 0.0 copy-done.4
  27.0 0.0 copy-done.6
  27.0 0.0 copy-done.8
  27.0 0.0 copy-done.10
  27.0 0.0 copy-done.11
  27.0 14.0 %step.1 = (f32[4,256,2048]{2,1,0:T(8,128)}, f32[1024,128]{1,0:T(8,128)S(1)}) custom-call(f32[4,256,2048]{2,1,0:T(8,128)S(1)} %copy-done, bf16[3,256,2048]{2,1,0:T(8,128)(2,1)S(1)} %copy-done.1, bf16[4,240,2048]{2,1,0:T(8,128)(2,1)S(1)} %flux.1, bf16[768,256]{1,0:T(8,128)(2,1)S(1)} %copy-done.4, bf16[216,256]{1,0:T(8,128)(2,1)S(1)} %bitcast.4, ...), custom_call_target="tpu_custom_call" | custom-call | tf_op jit(solution)/shard_map/step/pallas_call | solution.py:362
  41.0 13.5 %sum.1 = f32[32,128]{1,0:T(8,128)S(1)} custom-call(f32[1024,128]{1,0:T(8,128)S(1)} %get-tuple-element.5.partial), custom_call_target="tpu_custom_call" | custom-call | tf_op jit(solution)/shard_map/sum/pallas_call | solution.py:385
  54.5 0.6 %copy.16 = f32[32,128]{1,0:T(8,128)} copy(f32[32,128]{1,0:T(8,128)S(1)} %sum.1) | data formatting | bytes 32768
Async XLA Ops:
  0.6 26.3 %copy-start = (f32[4,256,2048]{2,1,0:T(8,128)S(1)}, f32[4,256,2048]{2,1,0:T(8,128)}, u32[]{:S(2)}) copy-start(f32[4,256,2048]{2,1,0:T(8,128)} %adjoint.3) | copy-start | bytes 25165828
  0.6 26.3 %copy-start.1 = (bf16[3,256,2048]{2,1,0:T(8,128)(2,1)S(1)}, bf16[3,256,2048]{2,1,0:T(8,128)(2,1)}, u32[]{:S(2)}) copy-start(bf16[3,256,2048]{2,1,0:T(8,128)(2,1)} %velocity.1) | copy-start | bytes 9437188
  0.7 1.3 %copy-start.2 = (bf16[216,2048]{1,0:T(8,128)(2,1)S(1)}, bf16[216,2048]{1,0:T(8,128)(2,1)}, u32[]{:S(2)}) copy-start(bf16[216,2048]{1,0:T(8,128)(2,1)} %speed.1) | copy-start | bytes 2654212
  2.0 1.5 %copy-start.3 = (bf16[240,216]{1,0:T(8,128)(2,1)S(1)}, bf16[240,216]{1,0:T(8,128)(2,1)}, u32[]{:S(2)}) copy-start(bf16[240,216]{1,0:T(8,128)(2,1)} %constant.5.clone.spread) | copy-start | bytes 311044
  3.4 1.6 %copy-start.5 = (bf16[240,256]{1,0:T(8,128)(2,1)S(1)}, bf16[240,256]{1,0:T(8,128)(2,1)}, u32[]{:S(2)}) copy-start(bf16[240,256]{1,0:T(8,128)(2,1)} %constant.4.clone.select) | copy-start | bytes 368644
  5.1 0.8 %copy-start.7 = (s32[6,2048]{1,0:T(8,128)S(1)}, s32[6,2048]{1,0:T(8,128)}, u32[]{:S(2)}) copy-start(s32[6,2048]{1,0:T(8,128)} %neighbours.1) | copy-start | bytes 147460
  5.9 0.7 %copy-start.9 = (s32[4,512]{1,0:T(4,128)S(1)}, s32[4,512]{1,0:T(4,128)}, u32[]{:S(2)}) copy-start(s32[4,512]{1,0:T(4,128)} %sub_sends.1) | copy-start | bytes 24580
  6.6 0.7 %copy-start.12 = (s32[2,256]{1,0:T(2,128)S(1)}, s32[2,256]{1,0:T(2,128)}, u32[]{:S(2)}) copy-start(s32[2,256]{1,0:T(2,128)} %group_sends.1) | copy-start | bytes 6148
  7.3 19.7 %copy-start.4 = (bf16[768,256]{1,0:T(8,128)(2,1)S(1)}, bf16[768,256]{1,0:T(8,128)(2,1)}, u32[]{:S(2)}) copy-start(bf16[768,256]{1,0:T(8,128)(2,1)} %derivatives.1) | copy-start | bytes 1179652
  7.3 19.7 %copy-start.6 = (bf16[256,216]{0,1:T(8,128)(2,1)S(1)}, bf16[256,216]{0,1:T(8,128)(2,1)}, u32[]{:S(2)}) copy-start(bf16[256,216]{0,1:T(8,128)(2,1)} %param.17) | copy-start | bytes 331780
  7.3 19.7 %copy-start.8 = (bf16[256,32]{0,1:T(8,128)(2,1)S(1)}, bf16[256,32]{0,1:T(8,128)(2,1)}, u32[]{:S(2)}) copy-start(bf16[256,32]{0,1:T(8,128)(2,1)} %param.18) | copy-start | bytes 49156
  7.3 19.7 %copy-start.10 = (s32[2048]{0:T(1024)S(1)}, s32[2048]{0:T(1024)}, u32[]{:S(2)}) copy-start(s32[2048]{0:T(1024)} %param.22) | copy-start | bytes 24580
  7.3 19.7 %copy-start.11 = (s32[1024]{0:T(1024)S(1)}, s32[1024]{0:T(1024)}, u32[]{:S(2)}) copy-start(s32[1024]{0:T(1024)} %param.23) | copy-start | bytes 12292

commit v5 on v2

--- a/solution.py
+++ b/solution.py
@@ -77,10 +77,11 @@
 
 def flux_kernel(
     n_group, n_sub, cap,
-    adjoint, speed, neighbours, sub_sends, group_sends, select, spread,
+    adjoint, speed_hbm, neighbours_hbm, sub_sends_hbm, group_sends_hbm, select_hbm, spread_hbm,
     flux,
-    field, table, local, send_sub, recv_sub, send_group, recv_group, far_sub,
-    field_sem, sub_send_sem, sub_recv_sem, group_send_sem, group_recv_sem,
+    speed, neighbours, sub_sends, group_sends, select, spread,
+    field, table, local, send_sub, recv_sub, send_group, recv_group, far_sub, flux_out,
+    load_sem, flux_sem, field_sem, sub_send_sem, sub_recv_sem, group_send_sem, group_recv_sem,
 ):
     tiles, species = field.shape[0], field.shape[1]
     pad = select.shape[0] // FACES
@@ -94,13 +95,23 @@
         cols = pl.ds(pl.multiple_of(i * SPAN, SPAN), SPAN)
         return pltpu.make_async_copy(adjoint.at[:, :, cols], field.at[i], field_sem.at[i])
 
+    pairs = [
+        (select_hbm, select), (sub_sends_hbm, sub_sends), (group_sends_hbm, group_sends),
+        (neighbours_hbm, neighbours), (spread_hbm, spread), (speed_hbm, speed),
+    ]
+    loads = [pltpu.make_async_copy(a, b, load_sem.at[i]) for i, (a, b) in enumerate(pairs)]
+    loads[0].start()
     for i in range(tiles):
         field_copy(i).start()
+    for load in loads[1:]:
+        load.start()
 
     barrier = pltpu.get_barrier_semaphore()
     peers = [(g, lax.rem(q + d, n_sub)) for d in range(1, n_sub)] + [above, below]
     for peer in peers:
         pl.semaphore_signal(barrier, inc=1, device_id=peer, device_id_type=MESH)
+
+    loads[0].wait()
 
     def trace_tile(i, carry):
         for j in range(WIDE // SPAN):
@@ -116,6 +127,8 @@
 
     lax.fori_loop(0, tiles * SPAN // WIDE, trace_tile, 0)
 
+    for load in loads[1:]:
+        load.wait()
     low_half = lax.broadcasted_iota(jnp.int32, (block, 2 * cap), 1) < cap
     for axis_id in range(2):
         for c in range(n_sub * cap // WIDE):
@@ -182,6 +195,10 @@
             far_sub[t, (lane // SPAN) * block : (lane // SPAN + 1) * block,
                     lane % SPAN : lane % SPAN + 2 * cap] = both.astype(BF16)
 
+    def flux_copy(i):
+        cols = pl.ds(pl.multiple_of(i * WIDE, WIDE), WIDE)
+        return pltpu.make_async_copy(flux_out.at[i], flux.at[:, :, cols], flux_sem.at[i])
+
     def flux_tile(i, carry):
         cols = pl.ds(pl.multiple_of(i * WIDE, WIDE), WIDE)
         inside = WIDE // SPAN
@@ -207,10 +224,13 @@
             parts.append(wind * (outside - here.astype(F32)))
         for s in range(species):
             one = jnp.concatenate([p[s * pad : (s + 1) * pad] for p in parts], axis=0)
-            flux[s, :, cols] = one.astype(BF16)
+            flux_out[i, s] = one.astype(BF16)
+        flux_copy(i).start()
         return carry
 
     lax.fori_loop(0, elements // WIDE, flux_tile, 0)
+    for i in range(elements // WIDE):
+        flux_copy(i).wait()
 
 
 def step_kernel(
@@ -339,9 +359,13 @@
     flux = pl.pallas_call(
         functools.partial(flux_kernel, n_group, n_sub, cap),
         out_shape=jax.ShapeDtypeStruct((species, FACES * pad, elements), BF16),
-        in_specs=[pl.BlockSpec(memory_space=pl.ANY)] + [vmem] * 6,
-        out_specs=vmem,
+        in_specs=[pl.BlockSpec(memory_space=pl.ANY)] * 7,
+        out_specs=pl.BlockSpec(memory_space=pl.ANY),
         scratch_shapes=[
+            *[
+                pltpu.VMEM(a.shape, a.dtype)
+                for a in (face_speed, neighbours, sub_sends, group_sends, select, spread)
+            ],
             pltpu.VMEM((tiles, species, nodes, SPAN), F32),
             pltpu.VMEM((FACES, tiles * block, SPAN), BF16),
             pltpu.VMEM((FACES, block, elements), BF16),
@@ -350,6 +374,8 @@
             pltpu.VMEM((2, block, span_group), BF16),
             pltpu.VMEM((2, block, span_group), BF16),
             pltpu.VMEM((4, far_tiles * block, SPAN), BF16),
+            pltpu.VMEM((elements // WIDE, species, FACES * pad, WIDE), BF16),
+            dma((6,)), dma((elements // WIDE,)),
             dma((tiles,)), dma((n_sub,)), dma((n_sub,)), dma((2,)), dma((2,)),
         ],
         compiler_params=pltpu.CompilerParams(

time: 54.8 us -> 52.9 us (0.965)
  Pallas kernels: 52.5 us -> 50.7 us
    pallas_call x1, Pallas kernels: 22.7 us -> 20.9 us  [on_device(): pl.pallas_call(functools.partial(flux_kernel, n_group, n_sub, cap), out_s...]
where the time goes in v5:
time: 52.9 us; the launch traced here: 52.7 us
  Pallas kernels  50.7 us (96%)
  local copies, waits for them, and re-layouts  1.32 us (2%)
  between operations  0.65 us (1%)
    pallas_call x1, Pallas kernels, on_device(): pl.pallas_call(functools.partial(flux_kernel, n_group, n_sub, cap), out_s...  20.9 us
    pallas_call x1, Pallas kernels, on_device(): pl.pallas_call(step_kernel, grid=(elements // WIDE,), out_shape=(jax.Shap...  15.7 us
    pallas_call x1, Pallas kernels, on_device(): pl.pallas_call(functools.partial(sum_kernel, n_group, n_sub), out_shape=j...  14.2 us
    unnamed x1, local copies, waits for them, and re-layouts  1.32 us

profile of v5, /device:TPU:0, one launch (start us, length us, event | category | flops | bytes accessed | tf_op | source)
XLA Modules:
  0.0 52.7 jit_solution(9501119290856583950)
XLA Ops:
  0.6 20.9 %flux.1 = bf16[4,240,2048]{2,1,0:T(8,128)(2,1)} custom-call(f32[4,256,2048]{2,1,0:T(8,128)} %adjoint.3, bf16[216,2048]{1,0:T(8,128)(2,1)} %speed_hbm.1, s32[6,2048]{1,0:T(8,128)} %neighbours_hbm.1, s32[4,512]{1,0:T(4,128)} %sub_sends_hbm.1, s32[2,256]{1,0:T(2,128)} %group_sends_hbm.1, bf16[240,256]{1,0:T(8,128)(2,1)} %constant.4.clone.select_hbm, ...), custom_call_target="tpu_custom_call" | custom-call | tf_op jit(solution)/shard_map/flux/pallas_call | solution.py:359
  21.5 15.7 %step.1 = (f32[4,256,2048]{2,1,0:T(8,128)}, f32[1024,128]{1,0:T(8,128)}) custom-call(f32[4,256,2048]{2,1,0:T(8,128)} %adjoint.3, bf16[3,256,2048]{2,1,0:T(8,128)(2,1)} %velocity.1, bf16[4,240,2048]{2,1,0:T(8,128)(2,1)} %flux.1, bf16[768,256]{1,0:T(8,128)(2,1)} %derivatives.1, bf16[216,256]{1,0:T(8,128)(2,1)} %bitcast.4, bf16[32,256]{1,0:T(8,128)(2,1)} %bitcast.5, ...), custom_call_target="tpu_custom_call" | custom-call | tf_op jit(solution)/shard_map/step/pallas_call | solution.py:391
  37.2 14.2 %sum.1 = f32[32,128]{1,0:T(8,128)} custom-call(f32[1024,128]{1,0:T(8,128)} %get-tuple-element.5.partial_hbm), custom_call_target="tpu_custom_call" | custom-call | tf_op jit(solution)/shard_map/sum/pallas_call | solution.py:414
  51.4 1.3 %copy.16 = f32[32,128]{1,0:T(8,128)} copy(f32[32,128]{1,0:T(8,128)} %sum.1) | data formatting | bytes 32768
